TPU v7x, 512 devices: a whole 4x4x16 slice. The times are simulated.
512 devices in a mesh: row: 128 (over y, z, core), col: 4 (over x).
Axes of the slice: x: 4, y: 4, z: 16, core: 2. Of those that a mesh axis runs over, the one named last changes fastest.
Arguments:
- activations: float32 [4, 256, 6144], P(None, 'row', 'col'), may hold values from -500 to 500
- input_weight: float32 [3, 32, 128, 6144], P(None, None, 'row', 'col'), may hold values from -0.078125 to 0.078125
- output_weight: float32 [6144, 32, 128], P('row', 'col'), may hold values from -0.5 to 0.5
Outputs:
- block_output: float32 [4, 256, 6144], P(None, 'col', 'row')
All inputs are finite; a program needn't handle non-finite values.
Results may differ from a plain program's by a relative error of at most 0.00013.
Values sent between devices are 32-bit elements; how exact they have to be, the bound alone decides.
A program may use at most 64 MiB of HBM per device.

v0:
```python
import jax
import jax.numpy as jnp
from jax import lax
from jax.sharding import PartitionSpec as P

epsilon = 1e-06
highest = lax.Precision.HIGHEST


def normalize(values, totals, squares, model_width):
    center = totals / model_width
    spread = squares / model_width - center * center
    return (values - center) * lax.rsqrt(spread + epsilon)


def layer_norm(values):
    center = jnp.mean(values, -1, keepdims=True)
    spread = jnp.mean(values * values, -1, keepdims=True) - center * center
    return (values - center) * lax.rsqrt(spread + epsilon)


def shards(activations, input_weight, output_weight):
    row_count = lax.axis_size("row")
    col_count = lax.axis_size("col")
    images = activations.shape[0]
    patches = activations.shape[1] * row_count
    model_width = activations.shape[2] * col_count
    head_count = input_weight.shape[1]
    feature_count = input_weight.shape[2]
    head_dim = feature_count * row_count
    splits = max(1, row_count * col_count // (images * head_count))
    query_span = patches // splits
    totals, squares = lax.psum(
        (
            jnp.sum(activations, -1, keepdims=True),
            jnp.sum(activations * activations, -1, keepdims=True),
        ),
        "col",
    )
    normed = normalize(activations, totals, squares, model_width)
    weight_table = input_weight.reshape(-1, input_weight.shape[3])
    partial_value = jnp.einsum(
        "ipe,ce->ipc",
        lax.all_gather(normed, "row", axis=1, tiled=True),
        weight_table,
        precision=highest,
    )
    partial_value = partial_value.reshape(images, patches, 3, head_count, feature_count)
    triples = lax.psum_scatter(partial_value, "col", scatter_dimension=3, tiled=True)
    group_heads = head_count // col_count
    item_total = images * group_heads * splits
    queries = jnp.transpose(triples[:, :, 0], (0, 2, 1, 3)).reshape(
        item_total, query_span, feature_count
    )
    keyvals = jnp.transpose(triples[:, :, 1:], (0, 3, 2, 1, 4))
    keyvals = jnp.broadcast_to(
        keyvals[:, :, None], (images, group_heads, splits, 2, patches, feature_count)
    )
    keyvals = keyvals.reshape(item_total, 2 * patches, feature_count)
    queries, keyvals = (
        lax.all_to_all(queries, "row", split_axis=0, concat_axis=2, tiled=True),
        lax.all_to_all(keyvals, "row", split_axis=0, concat_axis=2, tiled=True),
    )
    normed_queries = layer_norm(queries)
    normed_keys = layer_norm(keyvals[:, :patches])
    values = keyvals[:, patches:]
    scores = jnp.einsum(
        "kqd,kpd->kqp", normed_queries, normed_keys, precision=highest
    ) * head_dim ** (-0.5)
    weights = jnp.exp(scores)
    weights = weights / jnp.sum(weights, -1, keepdims=True)
    attended = jnp.einsum("kqp,kpd->kqd", weights, values, precision=highest)
    output_width = output_weight.shape[0]
    shard_rows = lax.all_gather(attended, "row", axis=0, tiled=True)
    item_count = shard_rows.shape[0]
    positions = jnp.arange(item_count, dtype=jnp.int32)
    head_index = positions // splits % group_heads
    onehot = (head_index[:, None] == jnp.arange(group_heads, dtype=jnp.int32)[None, :]).astype(
        jnp.float32
    )
    tables = jnp.einsum("kh,nhd->knd", onehot, output_weight, precision=highest)
    projected = jnp.einsum("kqd,knd->kqn", shard_rows, tables, precision=highest)
    partial_out = projected.reshape(images, group_heads, splits, query_span, output_width)
    partial_out = jnp.sum(partial_out, 1).reshape(images, patches, output_width)
    return lax.psum_scatter(partial_out, "col", scatter_dimension=1, tiled=True)


def solution(mesh):
    return jax.shard_map(
        shards,
        mesh=mesh,
        in_specs=(P(None, "row", "col"), P(None, None, "row", "col"), P("row", "col", None)),
        out_specs=P(None, "col", "row"),
        check_vma=False,
    )
```

profile of v0, /device:TPU:1, one launch (start us, length us, event | category | flops | bytes accessed | tf_op | source)
XLA Modules:
  0.0 444.0 jit_solution(5202862795916317084)
XLA Ops:
  6.5 0.0 copy-start
  6.5 0.0 all-gather.4.cloned.1.call-start
  6.5 1.0 fusion.28
  7.5 0.1 copy.17
  7.6 0.1 copy.19
  7.7 9.3 %all-reduce = (f32[4,2,1]{0,1,2:T(2,128)S(1)}, f32[4,2,1]{0,1,2:T(2,128)S(1)}) all-reduce(f32[4,2,1]{0,1,2:T(2,128)S(1)} %bitcast.70, f32[4,2,1]{0,1,2:T(2,128)S(1)} %bitcast.69), channel_id=1, replica_groups=mesh['row'=128,'col'=4] {'col'}, use_global_device_ids=true, to_apply=%region_3.0 | all-reduce | flops 16 | bytes 128 | tf_op jit(solution)/shard_map/psum | solution.py:33
  17.0 1.5 fusion.19
  18.5 0.0 all-gather.4.cloned.1.call-update
  18.5 0.0 reduce-scatter.5.cloned.1.call-start
  18.5 149.4 %all-gather.4.cloned.1.call-done = f32[4,256,1536]{2,0,1:T(4,128)} async-done(((f32[4,2,1536]{2,0,1:T(4,128)}), f32[4,256,1536]{2,0,1:T(4,128)}) %all-gather.4.cloned.1.call-update) | async-done | bytes 6291472 | tf_op jit(solution)/shard_map/all_gather | solution.py:44
  168.0 11.3 %fusion.4 = f32[4,256,3,32,1]{1,3,2,0,4:T(8,128)} fusion(f32[4,256,1536,1]{2,0,1,3:T(4,128)} %bitcast.61, f32[3,32,1,1536]{3,2,1,0:T(1,128)} %param.4), kind=kOutput, calls=%fused_computation.4 | convolution fusion | flops 1811939328 | bytes 7274496 | tf_op jit(solution)/shard_map/ipe,ce->ipc/dot_general | solution.py:42
  179.3 0.0 reduce-scatter.5.cloned.1.call-update
  179.3 21.0 %reduce-scatter.5.cloned.1.call-done = f32[4,256,3,8,1]{1,3,2,0,4:T(8,128)} async-done(((f32[4,256,3,32,1]{1,3,2,0,4:T(8,128)}), f32[4,256,3,8,1]{1,3,2,0,4:T(8,128)}) %reduce-scatter.5.cloned.1.call-update) | async-done | bytes 98320 | tf_op jit(solution)/shard_map/reduce_scatter | solution.py:49
  200.3 0.8 slice_bitcast_fusion.1
  201.0 0.7 reshape.203
  201.8 18.7 %all-to-all-start = ((f32[128,64,1]{1,2,0:T(1,128)}), f32[128,64,1]{1,2,0:T(1,128)S(1)}, u32[]{:S(2)}, u32[]{:S(2)}) async-start(f32[128,64,1]{1,2,0:T(1,128)} %bitcast.8), calls=%async_computation.1 | async-start | bytes 131072 | tf_op jit(solution)/shard_map/all_to_all | solution.py:61
  220.5 0.9 slice_bitcast_fusion
  221.3 0.1 broadcast_in_dim.26
  221.4 1.1 broadcast_in_dim.27
  222.5 12.9 %all-to-all-done = f32[128,64,1]{1,2,0:T(1,128)S(1)} async-done(((f32[128,64,1]{1,2,0:T(1,128)}), f32[128,64,1]{1,2,0:T(1,128)S(1)}, u32[]{:S(2)}, u32[]{:S(2)}) %all-to-all-start) | async-done | bytes 32800 | tf_op jit(solution)/shard_map/all_to_all | solution.py:61
  235.4 6.6 %all-to-all-start.1 = ((f32[128,512,1]{1,2,0:T(1,128)}), f32[128,512,1]{1,2,0:T(1,128)S(1)}, u32[]{:S(2)}, u32[]{:S(2)}) async-start(f32[128,512,1]{1,2,0:T(1,128)} %broadcast_in_dim.27), calls=%async_computation.2 | async-start | bytes 524288 | tf_op jit(solution)/shard_map/all_to_all | solution.py:62
  242.0 0.2 all-gather.6.cloned.1.call-start
  242.2 0.2 reduce_sum.74
  242.4 22.2 %all-to-all-done.1 = f32[128,512,1]{1,2,0:T(1,128)S(1)} async-done(((f32[128,512,1]{1,2,0:T(1,128)}), f32[128,512,1]{1,2,0:T(1,128)S(1)}, u32[]{:S(2)}, u32[]{:S(2)}) %all-to-all-start.1) | async-done | bytes 262176 | tf_op jit(solution)/shard_map/all_to_all | solution.py:62
  264.6 0.2 slice_reduce_fusion
  264.8 0.2 subtract_multiply_fusion
  265.0 0.4 fusion.29
  265.4 0.9 fusion.10
  266.3 0.0 all-gather.6.cloned.1.call-update
  266.4 0.0 reduce-scatter.7.cloned.1.call-start
  266.4 0.0 copy-done
  266.4 1.4 fusion.24
  267.9 130.9 %all-gather.6.cloned.1.call-done = f32[8192,128]{1,0:T(8,128)} async-done(((f32[64,128]{1,0:T(8,128)}), f32[8192,128]{1,0:T(8,128)}) %all-gather.6.cloned.1.call-update) | async-done | bytes 4194320 | tf_op jit(solution)/shard_map/all_gather | solution.py:74
  398.8 11.9 %fusion.2 = f32[128,64,48]{1,2,0:T(8,128)} fusion(f32[128,64,128]{2,1,0:T(8,128)} %bitcast.62, f32[128,48,128]{2,0,1:T(8,128)S(1)} %fusion.24), kind=kOutput, calls=%fused_computation.2 | convolution fusion | flops 603979776 | bytes 8912896 | tf_op jit(solution)/shard_map/kqd,knd->kqn/dot_general | solution.py:82
  410.7 2.2 reduce_sum.79
  412.9 0.2 copy.30
  413.2 1.0 reshape.213
  414.1 0.0 reduce-scatter.7.cloned.1.call-update
  414.2 21.6 %reduce-scatter.7.cloned.1.call-done = f32[64,192]{1,0:T(8,128)} async-done(((f32[256,192]{1,0:T(8,128)}), f32[64,192]{1,0:T(8,128)}) %reduce-scatter.7.cloned.1.call-update) | async-done | bytes 49168
  435.8 1.0 reshape.214
  436.7 0.7 copy.29
  (6 shorter events, 0.1 us)
Async XLA Ops:
  6.5 259.9 %copy-start = (f32[48,8,128]{2,1,0:T(8,128)S(1)}, f32[48,8,128]{2,1,0:T(8,128)}, u32[]{:S(2)}) copy-start(f32[48,8,128]{2,1,0:T(8,128)} %param.5) | copy-start | bytes 589828
  6.5 161.4 %all-gather.4.cloned.1.call-start = ((), (), s32[]{:S(2)}) async-start(), calls=%async_computation.4 | async-start | bytes 6340608 | tf_op jit(solution)/shard_map/all_gather | solution.py:44
  18.5 181.8 %reduce-scatter.5.cloned.1.call-start = ((), (), s32[]{:S(2)}) async-start(), calls=%async_computation.5 | async-start | bytes 491520 | tf_op jit(solution)/shard_map/reduce_scatter | solution.py:49
  201.8 33.7 %all-to-all-start = ((f32[128,64,1]{1,2,0:T(1,128)}), f32[128,64,1]{1,2,0:T(1,128)S(1)}, u32[]{:S(2)}, u32[]{:S(2)}) async-start(f32[128,64,1]{1,2,0:T(1,128)} %bitcast.8), calls=%async_computation.1 | async-start | bytes 131072 | tf_op jit(solution)/shard_map/all_to_all | solution.py:61
  235.4 29.2 %all-to-all-start.1 = ((f32[128,512,1]{1,2,0:T(1,128)}), f32[128,512,1]{1,2,0:T(1,128)S(1)}, u32[]{:S(2)}, u32[]{:S(2)}) async-start(f32[128,512,1]{1,2,0:T(1,128)} %broadcast_in_dim.27), calls=%async_computation.2 | async-start | bytes 524288 | tf_op jit(solution)/shard_map/all_to_all | solution.py:62
  242.0 156.8 %all-gather.6.cloned.1.call-start = ((), (), s32[]{:S(2)}) async-start(), calls=%async_computation.6 | async-start | bytes 4227072 | tf_op jit(solution)/shard_map/all_gather | solution.py:74
  266.4 169.4 %reduce-scatter.7.cloned.1.call-start = ((), (), s32[]{:S(2)}) async-start(), calls=%async_computation.7 | async-start | bytes 327680
Sparse Core Ops, SparseCore 0:
  18.6 149.3 all-gather.3
  179.4 20.8 reduce-scatter.4
  266.5 132.2 all-gather.5
  414.3 21.4 reduce-scatter.6
where the time goes:
time: 446 us; the launch traced here: 444 us
  waiting for transfers between devices  358 us (80%)
  matrix products  25.9 us (6%)
  starting transfers between devices  25.6 us (6%)
  between operations  13.2 us (3%)
  blocking collectives  9.27 us (2%)
  local copies, waits for them, and re-layouts  6.59 us (1%)
  other arithmetic  5.3 us (1%)
    all_gather x1, waiting for transfers between devices, shards(): lax.all_gather(normed, 'row', axis=1, tiled=True)  149 us
    all_gather x1, waiting for transfers between devices, shards(): shard_rows = lax.all_gather(attended, 'row', axis=0, tiled=True)  131 us
    all_to_all x1, waiting for transfers between devices, shards(): lax.all_to_all(keyvals, 'row', split_axis=0, concat_axis=2, tiled=True)  22.2 us
    unnamed x5, waiting for transfers between devices  21.7 us
    reduce_scatter x1, waiting for transfers between devices, shards(): lax.psum_scatter(partial_value, 'col', scatter_dimension=3, tiled=True)  21 us
    all_to_all x1, starting transfers between devices, shards(): lax.all_to_all(queries, 'row', split_axis=0, concat_axis=2, tiled=True)  18.7 us
    all_to_all x1, waiting for transfers between devices, shards(): lax.all_to_all(queries, 'row', split_axis=0, concat_axis=2, tiled=True)  12.9 us
    dot_general x1, matrix products, shards(): jnp.einsum('kqd,knd->kqn', shard_rows, tables, precision=highest)  11.9 us
  transfers between devices with their start and end apart: 6, of which 6 were waited for; matrix products, arithmetic and copies ran while one was open for 1% of the time, Pallas kernels for 0%

commit v1 on v0

v1 whole, which is shorter than its diff:
```python
import jax
import jax.numpy as jnp
from jax import lax
from jax.experimental import pallas as pl
from jax.experimental.pallas import tpu as pltpu
from jax.sharding import PartitionSpec as P

MESH = pl.DeviceIdType.MESH
EPS = 1e-06
HIGHEST = lax.Precision.HIGHEST
F32 = jnp.float32
BF16 = jnp.bfloat16

NX, NY, NZ, NC = 4, 4, 16, 2
LANE = 128
TILES = 48
KT = TILES // NX
R1, R2 = 64, 32
HEADS = 32
NZZ = 8
A1 = 80
FEAT = 96
NOUT = 48


def split(x):
    hi = x.astype(BF16)
    return hi, (x - hi.astype(F32)).astype(BF16)


def kernel(act, w, ow, out, *scratch):
    (chunk, g1, g2, wb, whl, ghl, ob, owhl, msg, rcv, kv, att, fs, fr, acc,
     act_s, act_r, w_s, w_r, wf_s, wf_r, wc_s, wc_r, o_s, o_r, of_s, of_r, oc_s, oc_r,
     s1, r1, s2, r2, sy, ry, syh, ryh, sp, rp, a2a_s, a2a_r, kv_s, kv_r,
     t1, u1, t2, u2, ty, uy, tyh, uyh, tp, up, f_s, f_r, loc) = scratch
    row = lax.axis_index("row")
    x = lax.axis_index("col")
    c = row % 2
    z = row // 2 % NZ
    y = row // (2 * NZ)
    oc = 1 - c

    def dev(yy, zz, cc, xx):
        return ((yy * NZ + zz) * 2 + cc, xx)

    def wrap(v, n):
        return (v + n) % n

    def remote(src, dst, ssem, rsem, where):
        copy = pltpu.make_async_remote_copy(
            src_ref=src, dst_ref=dst, send_sem=ssem, recv_sem=rsem, device_id=where, device_id_type=MESH
        )
        copy.start()

    def wait(ref, sem):
        pltpu.make_async_copy(ref, ref, sem).wait()

    xp, xm, xo = wrap(x + 1, NX), wrap(x - 1, NX), wrap(x + 2, NX)
    yp, ym, yo = wrap(y + 1, NY), wrap(y - 1, NY), wrap(y + 2, NY)
    zp, zm = wrap(z + 1, NZ), wrap(z - 1, NZ)

    bar = pltpu.get_barrier_semaphore()
    me = y * NZ + z

    def greet(k, carry):
        other = (me + k) % (NY * NZ)
        pl.semaphore_signal(bar, inc=1, device_id=(other * 2 + c, x), device_id_type=MESH)
        return carry

    lax.fori_loop(1, NY * NZ, greet, 0)
    for dx in range(NX):
        for dc in range(NC):
            if dx or dc:
                pl.semaphore_signal(
                    bar, inc=1, device_id=dev(y, z, (c + dc) % 2, (x + dx) % NX), device_id_type=MESH
                )
    pl.semaphore_wait(bar, NY * NZ - 1 + NX * NC - 1)

    for i in range(1, NX):
        xt = (x + i) % NX
        remote(act.at[xt], chunk.at[x], act_s.at[i], act_r.at[i], dev(y, z, c, xt))

    def gather_start(src, buf, half, ss, rs, cs, cr, ls):
        for q, (first, target) in enumerate(((0, xp), (1, xm))):
            for p in (first, 1 - first):
                rows = pl.ds(p * half, half)
                remote(src.at[rows], buf.at[c, x, rows], ss.at[q, p], rs.at[q, p], dev(y, z, c, target))
        for p in range(2):
            rows = pl.ds(p * half, half)
            remote(src.at[rows], buf.at[c, x, rows], cs.at[p], cr.at[p], dev(y, z, oc, x))
        pltpu.make_async_copy(src, buf.at[c, x], ls).start()

    def gather_pass(buf, half, q, p, ss, rs, fs_, fr_, cs, cr):
        origin = xm if q == 0 else xp
        rows = pl.ds(p * half, half)
        piece = buf.at[c, origin, rows]
        wait(piece, rs.at[q, p])
        if p == q:
            remote(piece, piece, fs_.at[q], fr_.at[q], dev(y, z, c, xp if q == 0 else xm))
        remote(piece, piece, cs.at[2 + 2 * q + p], cr.at[2 + 2 * q + p], dev(y, z, oc, x))

    def gather_last(buf, half, fr_, cs, cr):
        for q in range(2):
            rows = pl.ds(q * half, half)
            piece = buf.at[c, xo, rows]
            wait(piece, fr_.at[q])
            remote(piece, piece, cs.at[6 + q], cr.at[6 + q], dev(y, z, oc, x))

    def gather_core(buf, half, cr):
        for k, origin in enumerate((x, xm, xp, xo)):
            for p in range(2):
                wait(buf.at[oc, origin, pl.ds(p * half, half)], cr.at[2 * k + p])

    def gather_drain(src, buf, half, ss, fs_, cs):
        for q in range(2):
            for p in range(2):
                wait(src.at[pl.ds(p * half, half)], ss.at[q, p])
            wait(src.at[pl.ds(0, half)], fs_.at[q])
        for k in range(8):
            wait(src.at[pl.ds(0, half)], cs.at[k])

    WH = FEAT * KT // 2
    OH = NOUT * 8 // 2
    gather_start(w, wb, WH, w_s, w_r, wc_s, wc_r, loc.at[0])

    chunk[x] = act[x]
    for i in range(1, NX):
        wait(chunk.at[0], act_r.at[i])
    data = chunk[...].reshape(2 * TILES, LANE)
    odd = lax.broadcasted_iota(jnp.int32, (2 * TILES, LANE), 0) % 2 == 1
    square = data * data
    zero = jnp.zeros_like(data)

    def total(v):
        return jnp.sum(jnp.sum(v, 0, keepdims=True), 1, keepdims=True)

    width = TILES * LANE
    center = [total(jnp.where(odd, data, zero) if b else jnp.where(odd, zero, data)) / width for b in range(2)]
    second = [total(jnp.where(odd, square, zero) if b else jnp.where(odd, zero, square)) / width for b in range(2)]
    scale = [lax.rsqrt(second[b] - center[b] * center[b] + EPS) for b in range(2)]
    normed = (data - jnp.where(odd, center[1], center[0])) * jnp.where(odd, scale[1], scale[0])
    g1[y, z] = normed[:R1]
    g2[y, z] = normed[R1:]

    def z1(d, s, half=False):
        slot = wrap(z - (s - 1), NZ) if d == 0 else wrap(z + (s - 1), NZ)
        piece = g1.at[y, slot, pl.ds(d * (R1 // 2), R1 // 2)] if half else g1.at[y, slot]
        remote(piece, piece, s1.at[d, s - 1], r1.at[d, s - 1], dev(y, zp if d == 0 else zm, c, x))

    def z2(d, s, half=False):
        slot = wrap(z - (s - 1), NZ) if d == 0 else wrap(z + (s - 1), NZ)
        piece = g2.at[:, slot, pl.ds(d * (R2 // 2), R2 // 2)] if half else g2.at[:, slot]
        remote(piece, piece, s2.at[d, s - 1], r2.at[d, s - 1], dev(y, zp if d == 0 else zm, c, x))

    def y1(slot):
        piece = g1.at[y, slot]
        remote(piece, piece, sy.at[0, slot], ry.at[0, slot], dev(yp, z, c, x))
        remote(piece, piece, sy.at[1, slot], ry.at[1, slot], dev(ym, z, c, x))

    def y1pass(slot):
        wait(g1.at[ym, slot], ry.at[0, slot])
        piece = g1.at[ym, slot, pl.ds(0, R1 // 2)]
        remote(piece, piece, syh.at[0, slot], ryh.at[0, slot], dev(yp, z, c, x))
        wait(g1.at[yp, slot], ry.at[1, slot])
        piece = g1.at[yp, slot, pl.ds(R1 // 2, R1 // 2)]
        remote(piece, piece, syh.at[1, slot], ryh.at[1, slot], dev(ym, z, c, x))

    z1(0, 1)
    z1(1, 1)
    own2 = g2.at[y, z]
    for k, target in enumerate((yp, ym, yo)):
        remote(own2, own2, sp.at[k], rp.at[k], dev(target, z, c, x))
    y1(z)
    for k, origin in enumerate((ym, yp, yo)):
        wait(g2.at[origin, z], rp.at[k])
    z2(0, 1)
    z2(1, 1)

    def step(s, half=False):
        back, ahead = wrap(z - s, NZ), wrap(z + s, NZ)
        wait(g1.at[y, back], r1.at[0, s - 1])
        z1(0, s + 1, half)
        y1(back)
        wait(g1.at[y, ahead], r1.at[1, s - 1])
        z1(1, s + 1, half)
        y1(ahead)
        wait(g2.at[:, back], r2.at[0, s - 1])
        z2(0, s + 1, half)
        wait(g2.at[:, ahead], r2.at[1, s - 1])
        z2(1, s + 1, half)

    def wconv(d2, origin, p):
        def body(kt, carry):
            v = wb[d2, origin, pl.ds(p * WH + kt, FEAT // 2, stride=KT), :]
            hi, lo = split(v)
            lanes = pl.ds(pl.multiple_of(kt * LANE, LANE), LANE)
            at = pl.multiple_of(d2 * FEAT + p * (FEAT // 2), 16)
            whl[origin, pl.ds(at, FEAT // 2), lanes] = hi
            whl[origin, pl.ds(at + 2 * FEAT, FEAT // 2), lanes] = lo
            return carry

        lax.fori_loop(0, KT, body, 0)

    W = (w_s, w_r, wf_s, wf_r, wc_s, wc_r)
    O = (o_s, o_r, of_s, of_r, oc_s, oc_r)
    for s in range(1, 8):
        step(s, s == 7)
        if s == 1:
            y1pass(z)
        else:
            y1pass(wrap(z - (s - 1), NZ))
            y1pass(wrap(z + (s - 1), NZ))
        if s == 1:
            wait(w, loc.at[0])
            for p in range(2):
                wconv(c, x, p)
        if s == 2:
            gather_pass(wb, WH, 0, 0, *W)
            gather_pass(wb, WH, 1, 1, *W)
        if s == 3:
            wconv(c, xm, 0)
            wconv(c, xp, 1)
        if s == 5:
            gather_pass(wb, WH, 0, 1, *W)
            gather_pass(wb, WH, 1, 0, *W)
            gather_start(ow, ob, OH, o_s, o_r, oc_s, oc_r, loc.at[1])
        if s == 6:
            wconv(c, xm, 1)
            wconv(c, xp, 0)
    far = wrap(z + 8, NZ)
    wait(g1.at[y, far, pl.ds(0, R1 // 2)], r1.at[0, 7])
    wait(g1.at[y, far, pl.ds(R1 // 2, R1 // 2)], r1.at[1, 7])
    y1(far)
    y1pass(wrap(z - 7, NZ))
    y1pass(wrap(z + 7, NZ))
    gather_last(wb, WH, wf_r, wc_s, wc_r)
    wait(g2.at[:, far, pl.ds(0, R2 // 2)], r2.at[0, 7])
    wait(g2.at[:, far, pl.ds(R2 // 2, R2 // 2)], r2.at[1, 7])
    y1pass(far)
    for p in range(2):
        wconv(c, xo, p)
    gather_core(wb, WH, wc_r)
    for k in range(NX):
        for p in range(2):
            wconv(oc, k, p)
    gather_pass(ob, OH, 0, 0, *O)
    gather_pass(ob, OH, 1, 1, *O)

    def ywait(slot, carry):
        wait(g1.at[yo, slot, pl.ds(0, R1 // 2)], ryh.at[0, slot])
        wait(g1.at[yo, slot, pl.ds(R1 // 2, R1 // 2)], ryh.at[1, slot])
        return carry

    lax.fori_loop(0, NZ, ywait, 0)

    f1 = g1.reshape(NY * NZ * R1, LANE)
    f2 = g2.reshape(NY * NZ * R2, LANE)
    for t in range(TILES):
        for b in range(2):
            if 2 * t < R1:
                v = f1[pl.ds(2 * t + b, NY * NZ, stride=R1), :]
            else:
                v = f2[pl.ds(2 * t - R1 + b, NY * NZ, stride=R2), :]
            hi, lo = split(v)
            lanes = pl.ds(t % KT * LANE, LANE)
            ghl[t // KT, pl.ds(b * 64, 64), lanes] = hi
            ghl[t // KT, pl.ds(128 + b * 64, 64), lanes] = lo
    acc[...] = jnp.zeros_like(acc)

    def project(k, carry):
        acc[...] += lax.dot_general(
            whl[k], ghl[k], (((1,), (1,)), ((), ())), preferred_element_type=F32
        )
        return carry

    lax.fori_loop(0, NX, project, 0)
    full = acc[...]
    half_sum = full[:, :LANE] + full[:, LANE:]
    triples = half_sum[: 2 * FEAT] + half_sum[2 * FEAT :]

    msg[...] = jnp.zeros_like(msg)
    for d2 in range(2):
        for s in range(3):
            at = d2 * FEAT + s * HEADS
            msg[pl.ds(2 * s + d2, HEADS, stride=8), :] = triples[at : at + HEADS]

    def post(k, carry):
        h = (k + me // 2) % HEADS
        there = h // NZZ * NZ + h % NZZ * 2
        src = msg.at[pl.ds(pl.multiple_of(h * 8, 8), 8)]
        dst = rcv.at[pl.ds(pl.multiple_of(me * 8, 8), 8)]

        @pl.when(there != me)
        def _():
            remote(src, dst, a2a_s, a2a_r, (there * 2 + c, x))

        @pl.when(there == me)
        def _():
            pltpu.make_async_copy(src, dst, a2a_r).start()

        return carry

    lax.fori_loop(0, HEADS, post, 0)

    gather_pass(ob, OH, 0, 1, *O)
    gather_pass(ob, OH, 1, 0, *O)
    gather_last(ob, OH, of_r, oc_s, oc_r)
    wait(ow, loc.at[1])
    gather_core(ob, OH, oc_r)

    for d2 in range(2):
        for hq in range(NX):
            for j in range(8):
                v = ob[d2, hq, pl.ds(j, NOUT, stride=8), :]
                hi, lo = split(v)
                lanes = pl.ds(hq * LANE, LANE)
                owhl[j, pl.ds(d2 * NOUT, NOUT), lanes] = hi
                owhl[j, pl.ds(2 * NOUT + d2 * NOUT, NOUT), lanes] = lo

    even = z % 2 == 0
    zz0 = z // 2

    def norm_rows(v):
        m = jnp.sum(v, 0, keepdims=True) / LANE
        q = jnp.sum(v * v, 0, keepdims=True) / LANE - m * m
        return (v - m) * lax.rsqrt(q + EPS)

    @pl.when(even)
    def _():
        wait(rcv, a2a_r)

        def part(s):
            return jnp.concatenate([rcv[pl.ds(2 * s + d2, 64, stride=8), :] for d2 in range(2)], 0)

        kv[c, pl.ds(0, LANE)] = norm_rows(part(1))
        kv[c, pl.ds(LANE, LANE)] = part(2)
        mine = kv.at[c]
        remote(mine, mine, kv_s, kv_r, dev(y, z, oc, x))
        queries = norm_rows(part(0)) * (LANE ** -0.5)
        wait(kv.at[oc], kv_r)
        es = []
        for k in range(2):
            keys = kv[k, pl.ds(0, LANE)].T
            es.append(jnp.exp(jnp.dot(keys, queries, precision=HIGHEST, preferred_element_type=F32)))
        norm = jnp.sum(es[0], 0, keepdims=True) + jnp.sum(es[1], 0, keepdims=True)
        o = sum(
            jnp.dot(kv[k, pl.ds(LANE, LANE)], es[k] / norm, precision=HIGHEST, preferred_element_type=F32)
            for k in range(2)
        )
        for d2 in range(2):
            att[zz0, y, pl.ds(d2, 64, stride=2), :] = o[d2 * 64 : d2 * 64 + 64]

    A2 = LANE - A1

    def slot_of(d, k):
        return wrap(zz0 - k, NZZ) if d == 0 else wrap((z + 1) // 2 + k, NZZ)

    def b1(d, k, half=False):
        slot = slot_of(d, k)
        rows = pl.ds(d * (A1 // 2), A1 // 2) if half else pl.ds(0, A1)
        piece = att.at[slot, y, rows]
        remote(piece, piece, t1.at[d, k], u1.at[d, k], dev(y, zp if d == 0 else zm, c, x))

    def b2(d, k, half=False):
        slot = slot_of(d, k)
        rows = pl.ds(A1 + d * (A2 // 2), A2 // 2) if half else pl.ds(A1, A2)
        piece = att.at[slot, :, rows]
        remote(piece, piece, t2.at[d, k], u2.at[d, k], dev(y, zp if d == 0 else zm, c, x))

    def v1(slot):
        piece = att.at[slot, y, pl.ds(0, A1)]
        remote(piece, piece, ty.at[0, slot], uy.at[0, slot], dev(yp, z, c, x))
        remote(piece, piece, ty.at[1, slot], uy.at[1, slot], dev(ym, z, c, x))

    def v1pass(slot):
        wait(att.at[slot, ym, pl.ds(0, A1)], uy.at[0, slot])
        piece = att.at[slot, ym, pl.ds(0, A1 // 2)]
        remote(piece, piece, tyh.at[0, slot], uyh.at[0, slot], dev(yp, z, c, x))
        wait(att.at[slot, yp, pl.ds(0, A1)], uy.at[1, slot])
        piece = att.at[slot, yp, pl.ds(A1 // 2, A1 // 2)]
        remote(piece, piece, tyh.at[1, slot], uyh.at[1, slot], dev(ym, z, c, x))

    acc2 = acc.at[pl.ds(0, 4 * NOUT)]
    acc2[...] = jnp.zeros((4 * NOUT, 2 * LANE), F32)

    def finish(slot):
        wait(att.at[slot, yo, pl.ds(0, A1 // 2)], uyh.at[0, slot])
        wait(att.at[slot, yo, pl.ds(A1 // 2, A1 // 2)], uyh.at[1, slot])
        block = att[slot].reshape(NY * LANE, LANE)
        hi, lo = split(block)
        acc2[...] += jnp.dot(owhl[slot], jnp.concatenate([hi, lo], 1), preferred_element_type=F32)

    @pl.when(even)
    def _():
        b1(0, 0)
        b1(1, 0)
        own = att.at[zz0, y, pl.ds(A1, A2)]
        for k, target in enumerate((yp, ym, yo)):
            remote(own, own, tp.at[k], up.at[k], dev(target, z, c, x))
        v1(zz0)
        for k, origin in enumerate((ym, yp, yo)):
            wait(att.at[zz0, origin, pl.ds(A1, A2)], up.at[k])
        b2(0, 0)
        b2(1, 0)
        for k in range(1, 4):
            for d in range(2):
                slot = slot_of(d, k)
                wait(att.at[slot, y, pl.ds(0, A1)], u1.at[d, k - 1])
                b1(d, k)
                v1(slot)
            for d in range(2):
                slot = slot_of(d, k)
                wait(att.at[slot, :, pl.ds(A1, A2)], u2.at[d, k - 1])
                b2(d, k)
            if k == 1:
                v1pass(zz0)
                finish(zz0)
            else:
                for d in range(2):
                    v1pass(slot_of(d, k - 1))
                for d in range(2):
                    finish(slot_of(d, k - 1))
        slot = slot_of(0, 4)
        wait(att.at[slot, y, pl.ds(0, A1 // 2)], u1.at[0, 3])
        wait(att.at[slot, y, pl.ds(A1 // 2, A1 // 2)], u1.at[1, 3])
        v1(slot)
        wait(att.at[slot, :, pl.ds(A1, A2 // 2)], u2.at[0, 3])
        wait(att.at[slot, :, pl.ds(A1 + A2 // 2, A2 // 2)], u2.at[1, 3])
        for d in range(2):
            v1pass(slot_of(d, 3))
        v1pass(slot)
        for d in range(2):
            finish(slot_of(d, 3))
        finish(slot)

    @pl.when(jnp.logical_not(even))
    def _():
        for k in range(4):
            half = k == 3
            for d in range(2):
                slot = slot_of(d, k)
                wait(att.at[slot, y, pl.ds(0, A1)], u1.at[d, k])
                b1(d, k, half)
                v1(slot)
            for d in range(2):
                slot = slot_of(d, k)
                wait(att.at[slot, :, pl.ds(A1, A2)], u2.at[d, k])
                b2(d, k, half)
            if k:
                for d in range(2):
                    v1pass(slot_of(d, k - 1))
                for d in range(2):
                    finish(slot_of(d, k - 1))
        for d in range(2):
            v1pass(slot_of(d, 3))
        for d in range(2):
            finish(slot_of(d, 3))

    sums = acc2[...]
    sums = sums[:, :LANE] + sums[:, LANE:]
    sums = sums[: 2 * NOUT] + sums[2 * NOUT :]
    blocks = jnp.concatenate([sums, jnp.zeros((LANE - 2 * NOUT, LANE), F32)], 0).T
    for q in range(NX):
        for cc in range(NC):
            for b in range(2):
                at = b * 64 + q * 16
                fs[q, cc, pl.ds(b * 16, 16), pl.ds(0, NOUT)] = blocks[at : at + 16, cc * NOUT : cc * NOUT + NOUT]
    for dx in range(NX):
        for dc in range(NC):
            if dx or dc:
                tx, tc = (x + dx) % NX, (c + dc) % 2
                remote(fs.at[tx, tc], fr.at[x, c], f_s.at[dx, dc], f_r.at[dx, dc], dev(y, z, tc, tx))
    fr[x, c] = fs[x, c]
    for dx in range(NX):
        for dc in range(NC):
            if dx or dc:
                wait(fr.at[0, 0], f_r.at[dx, dc])
    for i in range(NX):
        for cc in range(NC):
            for b in range(2):
                out[i, pl.ds(2 * cc + b, 16, stride=4), :] = fr[i, cc, pl.ds(b * 16, 16), pl.ds(0, NOUT)]

    for i in range(1, NX):
        wait(chunk.at[0], act_s.at[i])
    gather_drain(w, wb, WH, w_s, wf_s, wc_s)
    gather_drain(ow, ob, OH, o_s, of_s, oc_s)
    for d in range(2):
        for s in range(8):
            wait(g1.at[0, 0, pl.ds(0, R1 // 2)] if s == 7 else g1.at[0, 0], s1.at[d, s])
            wait(g2.at[:, 0, pl.ds(0, R2 // 2)] if s == 7 else g2.at[:, 0], s2.at[d, s])
    for k in range(3):
        wait(own2, sp.at[k])

    def ydrain(slot, carry):
        for d in range(2):
            wait(g1.at[0, 0], sy.at[d, slot])
            wait(g1.at[0, 0, pl.ds(0, R1 // 2)], syh.at[d, slot])
        return carry

    lax.fori_loop(0, NZ, ydrain, 0)

    def vdrain(slot, carry):
        for d in range(2):
            wait(att.at[0, 0, pl.ds(0, A1)], ty.at[d, slot])
            wait(att.at[0, 0, pl.ds(0, A1 // 2)], tyh.at[d, slot])
        return carry

    lax.fori_loop(0, NZZ, vdrain, 0)
    for d in range(2):
        for k in range(3):
            wait(att.at[0, 0, pl.ds(0, A1)], t1.at[d, k])
            wait(att.at[0, :, pl.ds(A1, A2)], t2.at[d, k])

    @pl.when(even)
    def _():
        wait(msg.at[pl.ds(0, (HEADS - 1) * 8)], a2a_s)
        wait(kv.at[0], kv_s)
        for k in range(3):
            wait(att.at[0, 0, pl.ds(A1, A2)], tp.at[k])
        for d in range(2):
            wait(att.at[0, 0, pl.ds(0, A1)], t1.at[d, 3])
            wait(att.at[0, :, pl.ds(A1, A2)], t2.at[d, 3])

    @pl.when(jnp.logical_not(even))
    def _():
        wait(msg, a2a_s)
        for d in range(2):
            wait(att.at[0, 0, pl.ds(0, A1 // 2)], t1.at[d, 3])
            wait(att.at[0, :, pl.ds(A1, A2 // 2)], t2.at[d, 3])

    for dx in range(NX):
        for dc in range(NC):
            if dx or dc:
                wait(fs.at[0, 0], f_s.at[dx, dc])


def shards(activations, input_weight, output_weight):
    images = activations.shape[0]
    act = activations.reshape(images, 2, KT, LANE).transpose(0, 2, 1, 3).reshape(images, 2 * KT, LANE)
    w = input_weight.reshape(FEAT * KT, LANE)
    ow = output_weight.reshape(NOUT * 8, LANE)
    dma = pltpu.SemaphoreType.DMA
    vm = pltpu.VMEM
    scratch = [
        vm((NX, 2 * KT, LANE), F32),
        vm((NY, NZ, R1, LANE), F32),
        vm((NY, NZ, R2, LANE), F32),
        vm((NC, NX, FEAT * KT, LANE), F32),
        vm((NX, 4 * FEAT, KT * LANE), BF16),
        vm((NX, 2 * LANE, KT * LANE), BF16),
        vm((NC, NX, NOUT * 8, LANE), F32),
        vm((NZZ, 4 * NOUT, NY * LANE), BF16),
        vm((HEADS * 8, LANE), F32),
        vm((NY * NZ * 8, LANE), F32),
        vm((NC, 2 * LANE, LANE), F32),
        vm((NZZ, NY, LANE, LANE), F32),
        vm((NX, NC, 32, LANE), F32),
        vm((NX, NC, 32, LANE), F32),
        vm((4 * FEAT, 2 * LANE), F32),
        dma((NX,)), dma((NX,)),
        dma((2, 2)), dma((2, 2)), dma((2,)), dma((2,)), dma((8,)), dma((8,)),
        dma((2, 2)), dma((2, 2)), dma((2,)), dma((2,)), dma((8,)), dma((8,)),
        dma((2, 8)), dma((2, 8)), dma((2, 8)), dma((2, 8)),
        dma((2, NZ)), dma((2, NZ)), dma((2, NZ)), dma((2, NZ)),
        dma((3,)), dma((3,)),
        dma, dma, dma, dma,
        dma((2, 4)), dma((2, 4)), dma((2, 4)), dma((2, 4)),
        dma((2, NZZ)), dma((2, NZZ)), dma((2, NZZ)), dma((2, NZZ)),
        dma((3,)), dma((3,)),
        dma((NX, NC)), dma((NX, NC)),
        dma((2,)),
    ]
    return pl.pallas_call(
        kernel,
        out_shape=jax.ShapeDtypeStruct((NX, 64, NOUT), F32),
        in_specs=[
            pl.BlockSpec(memory_space=pltpu.VMEM),
            pl.BlockSpec(memory_space=pl.ANY),
            pl.BlockSpec(memory_space=pl.ANY),
        ],
        out_specs=pl.BlockSpec(memory_space=pltpu.VMEM),
        scratch_shapes=scratch,
        compiler_params=pltpu.CompilerParams(
            collective_id=0, has_side_effects=True, vmem_limit_bytes=48 * 1024 * 1024
        ),
    )(act, w, ow)


def solution(mesh):
    return jax.shard_map(
        shards,
        mesh=mesh,
        in_specs=(P(None, "row", "col"), P(None, None, "row", "col"), P("row", "col", None)),
        out_specs=P(None, "col", "row"),
        check_vma=False,
    )
```

time: 446 us -> 128 us (0.29)
  waiting for transfers between devices: 358 us -> 0 us
  Pallas kernels: 0 us -> 125 us
  matrix products: 25.9 us -> 0 us
  starting transfers between devices: 25.6 us -> 0 us
  between operations: 13.2 us -> 0.02 us
  blocking collectives: 9.27 us -> 0 us
  other arithmetic: 5.3 us -> 0 us
    all_gather x2 -> x0, waiting for transfers between devices: 280 us -> none  [the longest x1 149 us: shards(): lax.all_gather(normed, 'row', axis=1, tiled=True)]
    pallas_call x0 -> x1, Pallas kernels: none -> 125 us  [shards(): pl.pallas_call(kernel, out_shape=jax.ShapeDtypeStruct((NX, 64, NOUT), F32...]
    all_to_all x2 -> x0, waiting for transfers between devices: 35.1 us -> none  [the longest x1 22.2 us: shards(): lax.all_to_all(keyvals, 'row', split_axis=0, concat_axis=2, tiled=True)]
    dot_general x5 -> x0, matrix products: 25.9 us -> none  [the longest x1 11.9 us: shards(): jnp.einsum('kqd,knd->kqn', shard_rows, tables, precision=highest)]
    all_to_all x2 -> x0, starting transfers between devices: 25.2 us -> none  [the longest x1 18.7 us: shards(): lax.all_to_all(queries, 'row', split_axis=0, concat_axis=2, tiled=True)]
    unnamed x5 -> x0, waiting for transfers between devices: 21.7 us -> none
    reduce_scatter x1 -> x0, waiting for transfers between devices: 21 us -> none  [shards(): lax.psum_scatter(partial_value, 'col', scatter_dimension=3, tiled=True)]
    psum x1 -> x0, blocking collectives: 9.27 us -> none  [shards(): lax.psum((jnp.sum(activations, -1, keepdims=True), jnp.sum(activations *...]
  transfers between devices with their start and end apart: 6 -> 0, of which waited for: 6 -> 0; matrix products, arithmetic and copies ran while one was open for 1% -> 0% of each run, Pallas kernels for 0% -> 0%
where the time goes in v1:
time: 128 us; the launch traced here: 127 us
  Pallas kernels  125 us (98%)
  local copies, waits for them, and re-layouts  2.74 us (2%)
    pallas_call x1, Pallas kernels, shards(): pl.pallas_call(kernel, out_shape=jax.ShapeDtypeStruct((NX, 64, NOUT), F32...  125 us

profile of v1, /device:TPU:1, one launch (start us, length us, event | category | flops | bytes accessed | tf_op | source)
XLA Modules:
  0.0 127.5 jit_solution(14402638611909284879)
XLA Ops:
  0.0 0.0 copy-start.1
  0.0 0.9 reshape.12
  0.9 0.0 copy-done.1
  1.0 0.0 copy-start
  1.0 1.1 copy-done
  2.0 124.7 %shard_map.37 = f32[4,64,48]{2,1,0:T(8,128)S(1)} custom-call(f32[4,24,128]{2,1,0:T(8,128)S(1)} %bitcast.6, f32[1152,128]{1,0:T(8,128)S(1)} %bitcast.4, f32[384,128]{1,0:T(8,128)S(1)} %bitcast.5), custom_call_target="tpu_custom_call" | custom-call | tf_op jit(solution)/shard_map/pallas_call | solution.py:573
  126.7 0.7 copy.7
  (1 shorter events, 0.0 us)
Async XLA Ops:
  0.0 0.9 copy-start.1
  1.0 1.1 copy-start

commit v2 on v1

v2 whole, which is shorter than its diff:
```python
import jax
import jax.numpy as jnp
from jax import lax
from jax.experimental import pallas as pl
from jax.experimental.pallas import tpu as pltpu
from jax.sharding import PartitionSpec as P

MESH = pl.DeviceIdType.MESH
EPS = 1e-06
HIGHEST = lax.Precision.HIGHEST
F32 = jnp.float32
BF16 = jnp.bfloat16

NX, NY, NZ, NC = 4, 4, 16, 2
LANE = 128
TILES = 48
KT = TILES // NX
R1, R2 = 64, 32
HEADS = 32
NZZ = 8
A1 = 80
FEAT = 96
NOUT = 48


def split(x):
    hi = x.astype(BF16)
    return hi, (x - hi.astype(F32)).astype(BF16)


def kernel(act, w, ow, out, *scratch):
    (chunk, g1, g2, wb, whl, ghl, ob, owhl, msg, rcv, kv, att, fs, fr, acc,
     act_s, act_r, w_s, w_r, wf_r, wc_s, wc_r, o_s, o_r, of_r, oc_s, oc_r,
     z1_s, z2_s, y_s, h_s, c_s, p_s, r1, r2, ry, rh, rp, rc1, rc2,
     a2a_s, a2a_r, kv_s, kv_r, b_s, b_r, f_s, f_r, loc) = scratch
    row = lax.axis_index("row")
    x = lax.axis_index("col")
    c = row % 2
    z = row // 2 % NZ
    y = row // (2 * NZ)
    oc = 1 - c
    me = y * NZ + z
    near, far = c == 1, c == 0

    def dev(yy, zz, cc, xx):
        return ((yy * NZ + zz) * 2 + cc, xx)

    def wrap(v, n):
        return (v + n) % n

    def remote(src, dst, ssem, rsem, where):
        pltpu.make_async_remote_copy(
            src_ref=src, dst_ref=dst, send_sem=ssem, recv_sem=rsem, device_id=where, device_id_type=MESH
        ).start()

    def wait(ref, sem):
        pltpu.make_async_copy(ref, ref, sem).wait()

    flat = wb.reshape(NC * NX * FEAT * KT, LANE)

    def drain(sem, rows):
        wait(flat.at[pl.ds(0, rows)], sem)

    xp, xm, xo = wrap(x + 1, NX), wrap(x - 1, NX), wrap(x + 2, NX)
    yp, ym, yo = wrap(y + 1, NY), wrap(y - 1, NY), wrap(y + 2, NY)
    zp, zm = wrap(z + 1, NZ), wrap(z - 1, NZ)

    bar = pltpu.get_barrier_semaphore()

    def greet(k, carry):
        other = (me + k) % (NY * NZ)
        pl.semaphore_signal(bar, inc=1, device_id=(other * 2 + c, x), device_id_type=MESH)
        return carry

    lax.fori_loop(1, NY * NZ, greet, 0)
    for dx in range(NX):
        for dc in range(NC):
            if dx or dc:
                pl.semaphore_signal(
                    bar, inc=1, device_id=dev(y, z, (c + dc) % 2, (x + dx) % NX), device_id_type=MESH
                )
    pl.semaphore_wait(bar, NY * NZ - 1 + NX * NC - 1)

    for i in range(1, NX):
        xt = (x + i) % NX
        remote(act.at[xt], chunk.at[c, x], act_s.at[i], act_r.at[c, i], dev(y, z, 1, xt))

    @pl.when(far)
    def _():
        remote(act.at[x], chunk.at[0, x], act_s.at[0], act_r.at[0, 0], dev(y, z, 1, x))

    @pl.when(near)
    def _():
        pltpu.make_async_copy(act.at[x], chunk.at[1, x], act_r.at[1, 0]).start()

    def gather_start(src, buf, half, ss, rs, cs, cr, ls):
        for q, (first, target) in enumerate(((0, xp), (1, xm))):
            for p in (first, 1 - first):
                rows = pl.ds(p * half, half)
                remote(src.at[rows], buf.at[c, x, rows], ss, rs.at[q, p], dev(y, z, c, target))
        for p in range(2):
            rows = pl.ds(p * half, half)
            remote(src.at[rows], buf.at[c, x, rows], cs, cr.at[p], dev(y, z, oc, x))
        pltpu.make_async_copy(src, buf.at[c, x], ls).start()

    def gather_pass(buf, half, q, p, ss, rs, fr_, cs, cr):
        origin = xm if q == 0 else xp
        rows = pl.ds(p * half, half)
        piece = buf.at[c, origin, rows]
        wait(piece, rs.at[q, p])
        if p == q:
            remote(piece, piece, ss, fr_.at[q], dev(y, z, c, xp if q == 0 else xm))
        remote(piece, piece, cs, cr.at[2 + 2 * q + p], dev(y, z, oc, x))

    def gather_last(buf, half, fr_, cs, cr):
        for q in range(2):
            rows = pl.ds(q * half, half)
            piece = buf.at[c, xo, rows]
            wait(piece, fr_.at[q])
            remote(piece, piece, cs, cr.at[6 + q], dev(y, z, oc, x))

    def gather_core(buf, half, cr):
        for k, origin in enumerate((x, xm, xp, xo)):
            for p in range(2):
                wait(buf.at[oc, origin, pl.ds(p * half, half)], cr.at[2 * k + p])

    WH = FEAT * KT // 2
    OH = NOUT * 8 // 2
    W = (w_s, w_r, wf_r, wc_s, wc_r)
    O = (o_s, o_r, of_r, oc_s, oc_r)

    def wconv(d2, origin, p):
        def body(kt, carry):
            v = wb[d2, origin, pl.ds(p * WH + kt, FEAT // 2, stride=KT), :]
            hi, lo = split(v)
            lanes = pl.ds(pl.multiple_of(kt * LANE, LANE), LANE)
            at = pl.multiple_of(d2 * FEAT + p * (FEAT // 2), 16)
            whl[origin, pl.ds(at, FEAT // 2), lanes] = hi
            whl[origin, pl.ds(at + 2 * FEAT, FEAT // 2), lanes] = lo
            return carry

        lax.fori_loop(0, KT, body, 0)

    def weights(s):
        if s == 1:
            wait(w, loc.at[0])
            for p in range(2):
                wconv(c, x, p)
        if s == 2:
            gather_pass(wb, WH, 0, 0, *W)
            gather_pass(wb, WH, 1, 1, *W)
        if s == 3:
            wconv(c, xm, 0)
            wconv(c, xp, 1)
        if s == 4:
            for p in range(2):
                wait(wb.at[oc, x, pl.ds(p * WH, WH)], wc_r.at[p])
                wconv(oc, x, p)
        if s == 5:
            gather_pass(wb, WH, 0, 1, *W)
            gather_pass(wb, WH, 1, 0, *W)
            gather_start(ow, ob, OH, o_s, o_r, oc_s, oc_r, loc.at[1])
        if s == 6:
            wconv(c, xm, 1)
            wconv(c, xp, 0)
        if s == 7:
            for k, origin in ((1, xm), (2, xp)):
                for p in range(2):
                    wait(wb.at[oc, origin, pl.ds(p * WH, WH)], wc_r.at[2 * k + p])
                    wconv(oc, origin, p)
        if s == 8:
            gather_last(wb, WH, wf_r, wc_s, wc_r)
            for p in range(2):
                wconv(c, xo, p)
            for p in range(2):
                wait(wb.at[oc, xo, pl.ds(p * WH, WH)], wc_r.at[6 + p])
                wconv(oc, xo, p)
            gather_pass(ob, OH, 0, 0, *O)
            gather_pass(ob, OH, 1, 1, *O)

    gather_start(w, wb, WH, w_s, w_r, wc_s, wc_r, loc.at[0])

    def core(piece, sem):
        remote(piece, piece, c_s, sem, dev(y, z, 0, x))

    def back(d, s):
        return wrap(z - s, NZ) if d == 0 else wrap(z + s, NZ)

    def z1(cls, d, s, half=False):
        slot = back(d, s - 1)
        piece = g1.at[y, slot, cls, pl.ds(d * (R1 // 2), R1 // 2)] if half else g1.at[y, slot, cls]
        remote(piece, piece, z1_s, r1.at[cls, d, s - 1], dev(y, zp if d == 0 else zm, 1, x))

    def z2(cls, d, s, half=False):
        slot = back(d, s - 1)
        piece = g2.at[:, slot, cls, pl.ds(d * (R2 // 2), R2 // 2)] if half else g2.at[:, slot, cls]
        remote(piece, piece, z2_s, r2.at[cls, d, s - 1], dev(y, zp if d == 0 else zm, 1, x))

    def y1(slot):
        piece = g1.at[y, slot]
        remote(piece, piece, y_s, ry.at[0, slot], dev(yp, z, 1, x))
        remote(piece, piece, y_s, ry.at[1, slot], dev(ym, z, 1, x))
        core(g1.at[y, slot, 0], rc1.at[slot])

    def y1pass(slot):
        wait(g1.at[ym, slot], ry.at[0, slot])
        piece = g1.at[ym, slot, :, pl.ds(0, R1 // 2)]
        remote(piece, piece, h_s, rh.at[0, slot], dev(yp, z, 1, x))
        wait(g1.at[yp, slot], ry.at[1, slot])
        piece = g1.at[yp, slot, :, pl.ds(R1 // 2, R1 // 2)]
        remote(piece, piece, h_s, rh.at[1, slot], dev(ym, z, 1, x))
        core(g1.at[ym, slot, 0], rc1.at[slot])
        core(g1.at[yp, slot, 0], rc1.at[slot])

    def y1last(slot):
        wait(g1.at[yo, slot, :, pl.ds(0, R1 // 2)], rh.at[0, slot])
        wait(g1.at[yo, slot, :, pl.ds(R1 // 2, R1 // 2)], rh.at[1, slot])
        core(g1.at[yo, slot, 0], rc1.at[slot])

    @pl.when(near)
    def _():
        for cls in range(2):
            for i in range(NX):
                wait(chunk.at[0, 0], act_r.at[cls, i])
        for cls in range(2):
            data = chunk[cls]
            width = TILES * LANE

            def mean(v):
                return jnp.sum(jnp.sum(v, 0, keepdims=True), 2, keepdims=True) / width

            center = mean(data)
            scale = lax.rsqrt(mean(data * data) - center * center + EPS)
            normed = (data - center) * scale
            for t in range(TILES):
                v = normed[t // KT, :, t % KT * LANE : (t % KT + 1) * LANE]
                if 2 * t < R1:
                    g1[y, z, cls, pl.ds(2 * t, 2), :] = v
                else:
                    g2[y, z, cls, pl.ds(2 * t - R1, 2), :] = v
        for cls in range(2):
            for d in range(2):
                z1(cls, d, 1)
        own2 = g2.at[y, z]
        for k, target in enumerate((yp, ym, yo)):
            remote(own2, own2, p_s, rp.at[k], dev(target, z, 1, x))
        y1(z)
        for k, origin in enumerate((ym, yp, yo)):
            wait(g2.at[origin, z], rp.at[k])
        for cls in range(2):
            for d in range(2):
                z2(cls, d, 1)
        core(g2.at[:, z, 0], rc2.at[z])
        for s in range(1, 8):
            half = s == 7
            for cls in range(2):
                for d in range(2):
                    wait(g1.at[y, back(d, s), cls], r1.at[cls, d, s - 1])
                    z1(cls, d, s + 1, half)
            for d in range(2):
                y1(back(d, s))
            for cls in range(2):
                for d in range(2):
                    wait(g2.at[:, back(d, s), cls], r2.at[cls, d, s - 1])
                    z2(cls, d, s + 1, half)
            for d in range(2):
                core(g2.at[:, back(d, s), 0], rc2.at[back(d, s)])
            for d in range(1 if s == 1 else 2):
                y1pass(back(d, s - 1))
            if s > 1:
                for d in range(1 if s == 2 else 2):
                    y1last(back(d, s - 2))
            weights(s)
        opp = back(0, 8)
        for cls in range(2):
            for d in range(2):
                wait(g1.at[y, opp, cls, pl.ds(d * (R1 // 2), R1 // 2)], r1.at[cls, d, 7])
        y1(opp)
        for d in range(2):
            y1pass(back(d, 7))
        for cls in range(2):
            for d in range(2):
                wait(g2.at[:, opp, cls, pl.ds(d * (R2 // 2), R2 // 2)], r2.at[cls, d, 7])
        core(g2.at[:, opp, 0], rc2.at[opp])
        y1pass(opp)
        for d in range(2):
            y1last(back(d, 6))
        for d in range(2):
            y1last(back(d, 7))
        weights(8)
        y1last(opp)

    @pl.when(far)
    def _():
        for s in range(1, 9):
            weights(s)

        def arrive(slot, carry):
            wait(g1.at[:, slot, 0], rc1.at[slot])
            wait(g2.at[:, slot, 0], rc2.at[slot])
            return carry

        lax.fori_loop(0, NZ, arrive, 0)

    f1 = g1.reshape(NY * NZ * 2 * R1, LANE)
    f2 = g2.reshape(NY * NZ * 2 * R2, LANE)
    for t in range(TILES):
        for b in range(2):
            if 2 * t < R1:
                v = f1[pl.ds(c * R1 + 2 * t + b, NY * NZ, stride=2 * R1), :]
            else:
                v = f2[pl.ds(c * R2 + 2 * t - R1 + b, NY * NZ, stride=2 * R2), :]
            hi, lo = split(v)
            lanes = pl.ds(t % KT * LANE, LANE)
            ghl[t // KT, pl.ds(b * 64, 64), lanes] = hi
            ghl[t // KT, pl.ds(128 + b * 64, 64), lanes] = lo
    acc[...] = jnp.zeros_like(acc)

    def project(k, carry):
        acc[...] += lax.dot_general(
            whl[k], ghl[k], (((1,), (1,)), ((), ())), preferred_element_type=F32
        )
        return carry

    lax.fori_loop(0, NX, project, 0)
    full = acc[...]
    half_sum = full[:, :LANE] + full[:, LANE:]
    triples = half_sum[: 2 * FEAT] + half_sum[2 * FEAT :]

    msg[...] = jnp.zeros_like(msg)
    for d2 in range(2):
        for s in range(3):
            at = d2 * FEAT + s * HEADS
            msg[pl.ds(2 * s + d2, HEADS, stride=8), :] = triples[at : at + HEADS]

    def post(k, carry):
        h = (k + me // 2) % HEADS
        there = h // NZZ * NZ + h % NZZ * 2
        src = msg.at[pl.ds(pl.multiple_of(h * 8, 8), 8)]
        dst = rcv.at[pl.ds(pl.multiple_of(me * 8, 8), 8)]

        @pl.when(there != me)
        def _():
            remote(src, dst, a2a_s, a2a_r, (there * 2 + c, x))

        @pl.when(there == me)
        def _():
            pltpu.make_async_copy(src, dst, a2a_r).start()

        return carry

    lax.fori_loop(0, HEADS, post, 0)

    @pl.when(near)
    def _():
        drain(z1_s, 4 * (7 * R1 + R1 // 2))
        drain(z2_s, 4 * NY * (7 * R2 + R2 // 2))
        drain(y_s, NZ * 2 * 2 * R1)
        drain(h_s, NZ * 2 * R1)
        drain(c_s, NZ * NY * (R1 + R2))
        drain(p_s, 3 * 2 * R2)

    gather_pass(ob, OH, 0, 1, *O)
    gather_pass(ob, OH, 1, 0, *O)
    gather_last(ob, OH, of_r, oc_s, oc_r)
    wait(ow, loc.at[1])
    gather_core(ob, OH, oc_r)

    for d2 in range(2):
        for hq in range(NX):
            for j in range(8):
                v = ob[d2, hq, pl.ds(j, NOUT, stride=8), :]
                hi, lo = split(v)
                lanes = pl.ds(hq * LANE, LANE)
                owhl[j, pl.ds(d2 * NOUT, NOUT), lanes] = hi
                owhl[j, pl.ds(2 * NOUT + d2 * NOUT, NOUT), lanes] = lo

    even = z % 2 == 0
    odd = z % 2 == 1
    zz0 = z // 2

    def norm_rows(v):
        m = jnp.sum(v, 0, keepdims=True) / LANE
        q = jnp.sum(v * v, 0, keepdims=True) / LANE - m * m
        return (v - m) * lax.rsqrt(q + EPS)

    @pl.when(even)
    def _():
        wait(rcv, a2a_r)

        def part(s):
            return jnp.concatenate([rcv[pl.ds(2 * s + d2, 64, stride=8), :] for d2 in range(2)], 0)

        kv[c, pl.ds(0, LANE)] = norm_rows(part(1))
        kv[c, pl.ds(LANE, LANE)] = part(2)
        mine = kv.at[c]
        remote(mine, mine, kv_s, kv_r, dev(y, z, oc, x))
        queries = norm_rows(part(0)) * (LANE ** -0.5)
        wait(kv.at[oc], kv_r)
        es = []
        for k in range(2):
            keys = kv[k, pl.ds(0, LANE)].T
            es.append(jnp.exp(jnp.dot(keys, queries, precision=HIGHEST, preferred_element_type=F32)))
        norm = jnp.sum(es[0], 0, keepdims=True) + jnp.sum(es[1], 0, keepdims=True)
        o = sum(
            jnp.dot(kv[k, pl.ds(LANE, LANE)], es[k] / norm, precision=HIGHEST, preferred_element_type=F32)
            for k in range(2)
        )
        for d2 in range(2):
            att[zz0, y, c, pl.ds(d2, 64, stride=2), :] = o[d2 * 64 : d2 * 64 + 64]

    A2 = LANE - A1

    def slot_of(d, k):
        return wrap(zz0 - k, NZZ) if d == 0 else wrap((z + 1) // 2 + k, NZZ)

    def b1(cls, d, k, half=False):
        slot = slot_of(d, k)
        rows = pl.ds(d * (A1 // 2), A1 // 2) if half else pl.ds(0, A1)
        piece = att.at[slot, y, cls, rows]
        remote(piece, piece, z1_s, r1.at[cls, d, k], dev(y, zp if d == 0 else zm, 1, x))

    def b2(cls, d, k, half=False):
        slot = slot_of(d, k)
        rows = pl.ds(A1 + d * (A2 // 2), A2 // 2) if half else pl.ds(A1, A2)
        piece = att.at[slot, :, cls, rows]
        remote(piece, piece, z2_s, r2.at[cls, d, k], dev(y, zp if d == 0 else zm, 1, x))

    def v1(slot, own=False):
        piece = att.at[slot, y, :, pl.ds(0, A1)]
        remote(piece, piece, y_s, ry.at[0, slot], dev(yp, z, 1, x))
        remote(piece, piece, y_s, ry.at[1, slot], dev(ym, z, 1, x))
        if not own:
            core(att.at[slot, y, 0, pl.ds(0, A1)], rc1.at[slot])

    def v1pass(slot):
        wait(att.at[slot, ym, :, pl.ds(0, A1)], ry.at[0, slot])
        piece = att.at[slot, ym, :, pl.ds(0, A1 // 2)]
        remote(piece, piece, h_s, rh.at[0, slot], dev(yp, z, 1, x))
        wait(att.at[slot, yp, :, pl.ds(0, A1)], ry.at[1, slot])
        piece = att.at[slot, yp, :, pl.ds(A1 // 2, A1 // 2)]
        remote(piece, piece, h_s, rh.at[1, slot], dev(ym, z, 1, x))
        core(att.at[slot, ym, 0, pl.ds(0, A1)], rc1.at[slot])
        core(att.at[slot, yp, 0, pl.ds(0, A1)], rc1.at[slot])

    def v1last(slot):
        wait(att.at[slot, yo, :, pl.ds(0, A1 // 2)], rh.at[0, slot])
        wait(att.at[slot, yo, :, pl.ds(A1 // 2, A1 // 2)], rh.at[1, slot])
        core(att.at[slot, yo, 0, pl.ds(0, A1)], rc1.at[slot])

    acc2 = acc.at[pl.ds(0, 4 * NOUT)]
    acc2[...] = jnp.zeros((4 * NOUT, 2 * LANE), F32)

    def finish(slot, cls):
        block = att[slot, :, cls].reshape(NY * LANE, LANE)
        hi, lo = split(block)
        acc2[...] += jnp.dot(owhl[slot], jnp.concatenate([hi, lo], 1), preferred_element_type=F32)

    def z1wait(k, n):
        for cls in range(2):
            for d in range(2):
                wait(att.at[slot_of(d, k), y, cls, pl.ds(0, A1)], r1.at[cls, d, n])
                b1(cls, d, k, n == 3)
        for d in range(2):
            v1(slot_of(d, k))

    def z2wait(k, n):
        for cls in range(2):
            for d in range(2):
                wait(att.at[slot_of(d, k), :, cls, pl.ds(A1, A2)], r2.at[cls, d, n])
                b2(cls, d, k, n == 3)
        for d in range(2):
            core(att.at[slot_of(d, k), :, 0, pl.ds(A1, A2)], rc2.at[slot_of(d, k)])

    def lagged(slots):
        for slot in slots:
            v1pass(slot)
        for slot in slots:
            v1last(slot)
        for slot in slots:
            finish(slot, 1)

    @pl.when(near & even)
    def _():
        wait(att.at[zz0, y, 0], b_r)
        for cls in range(2):
            for d in range(2):
                b1(cls, d, 0)
        own = att.at[zz0, y, :, pl.ds(A1, A2)]
        for k, target in enumerate((yp, ym, yo)):
            remote(own, own, p_s, rp.at[k], dev(target, z, 1, x))
        v1(zz0, True)
        for k, origin in enumerate((ym, yp, yo)):
            wait(att.at[zz0, origin, :, pl.ds(A1, A2)], rp.at[k])
        for cls in range(2):
            for d in range(2):
                b2(cls, d, 0)
        for origin in (ym, yp, yo):
            core(att.at[zz0, origin, 0, pl.ds(A1, A2)], rc2.at[zz0])
        for k in range(1, 4):
            z1wait(k, k - 1)
            z2wait(k, k - 1)
            lagged([zz0] if k == 1 else [slot_of(0, k - 1), slot_of(1, k - 1)])
        slot = slot_of(0, 4)
        for cls in range(2):
            for d in range(2):
                wait(att.at[slot, y, cls, pl.ds(d * (A1 // 2), A1 // 2)], r1.at[cls, d, 3])
        v1(slot)
        for cls in range(2):
            for d in range(2):
                wait(att.at[slot, :, cls, pl.ds(A1 + d * (A2 // 2), A2 // 2)], r2.at[cls, d, 3])
        core(att.at[slot, :, 0, pl.ds(A1, A2)], rc2.at[slot])
        lagged([slot_of(0, 3), slot_of(1, 3)])
        lagged([slot])
        drain(p_s, 3 * 2 * A2)

    @pl.when(near & odd)
    def _():
        for k in range(4):
            z1wait(k, k)
            z2wait(k, k)
            if k:
                lagged([slot_of(0, k - 1), slot_of(1, k - 1)])
        lagged([slot_of(0, 3), slot_of(1, 3)])

    def from_near(slot):
        wait(att.at[slot, :, 0, pl.ds(0, A1)], rc1.at[slot])
        wait(att.at[slot, :, 0, pl.ds(A1, A2)], rc2.at[slot])
        finish(slot, 0)

    @pl.when(far & even)
    def _():
        own = att.at[zz0, y, 0]
        remote(own, own, b_s, b_r, dev(y, z, 1, x))
        wait(att.at[zz0, pl.ds(0, 3), 0, pl.ds(0, A1)], rc1.at[zz0])
        wait(att.at[zz0, pl.ds(0, 3), 0, pl.ds(A1, A2)], rc2.at[zz0])
        finish(zz0, 0)
        for k in range(1, 4):
            for d in range(2):
                from_near(slot_of(d, k))
        from_near(slot_of(0, 4))
        wait(own, b_s)

    @pl.when(far & odd)
    def _():
        for k in range(4):
            for d in range(2):
                from_near(slot_of(d, k))

    sums = acc2[...]
    sums = sums[:, :LANE] + sums[:, LANE:]
    sums = sums[: 2 * NOUT] + sums[2 * NOUT :]
    blocks = jnp.concatenate([sums, jnp.zeros((LANE - 2 * NOUT, LANE), F32)], 0).T
    for q in range(NX):
        for cc in range(NC):
            for b in range(2):
                at = b * 64 + q * 16
                fs[q, cc, pl.ds(b * 16, 16), pl.ds(0, NOUT)] = blocks[at : at + 16, cc * NOUT : cc * NOUT + NOUT]
    for dx in range(NX):
        for dc in range(NC):
            if dx or dc:
                tx, tc = (x + dx) % NX, (c + dc) % 2
                remote(fs.at[tx, tc], fr.at[x, c], f_s, f_r.at[dx, dc], dev(y, z, tc, tx))
    fr[x, c] = fs[x, c]
    for dx in range(NX):
        for dc in range(NC):
            if dx or dc:
                wait(fr.at[0, 0], f_r.at[dx, dc])
    for i in range(NX):
        for cc in range(NC):
            for b in range(2):
                out[i, pl.ds(2 * cc + b, 16, stride=4), :] = fr[i, cc, pl.ds(b * 16, 16), pl.ds(0, NOUT)]

    for i in range(1, NX):
        wait(chunk.at[0, 0], act_s.at[i])
    drain(w_s, 6 * WH)
    drain(wc_s, 8 * WH)
    drain(o_s, 6 * OH)
    drain(oc_s, 8 * OH)
    drain(f_s, 7 * 32)

    @pl.when(even)
    def _():
        drain(a2a_s, (HEADS - 1) * 8)
        wait(kv.at[0], kv_s)

    @pl.when(odd)
    def _():
        drain(a2a_s, HEADS * 8)

    @pl.when(far)
    def _():
        wait(chunk.at[0, 0], act_s.at[0])

    @pl.when(near)
    def _():
        drain(y_s, NZZ * 2 * 2 * A1)
        drain(h_s, NZZ * 2 * A1)

    @pl.when(near & even)
    def _():
        drain(z1_s, 16 * A1)
        drain(z2_s, 16 * NY * A2)
        drain(c_s, NZZ * NY * LANE - LANE)

    @pl.when(near & odd)
    def _():
        drain(z1_s, 14 * A1)
        drain(z2_s, 14 * NY * A2)
        drain(c_s, NZZ * NY * LANE)


def shards(activations, input_weight, output_weight):
    w = input_weight.reshape(FEAT * KT, LANE)
    ow = output_weight.reshape(NOUT * 8, LANE)
    dma = pltpu.SemaphoreType.DMA
    vm = pltpu.VMEM
    scratch = [
        vm((NC, NX, 2, KT * LANE), F32),
        vm((NY, NZ, NC, R1, LANE), F32),
        vm((NY, NZ, NC, R2, LANE), F32),
        vm((NC, NX, FEAT * KT, LANE), F32),
        vm((NX, 4 * FEAT, KT * LANE), BF16),
        vm((NX, 2 * LANE, KT * LANE), BF16),
        vm((NC, NX, NOUT * 8, LANE), F32),
        vm((NZZ, 4 * NOUT, NY * LANE), BF16),
        vm((HEADS * 8, LANE), F32),
        vm((NY * NZ * 8, LANE), F32),
        vm((NC, 2 * LANE, LANE), F32),
        vm((NZZ, NY, NC, LANE, LANE), F32),
        vm((NX, NC, 32, LANE), F32),
        vm((NX, NC, 32, LANE), F32),
        vm((4 * FEAT, 2 * LANE), F32),
        dma((NX,)), dma((NC, NX)),
        dma, dma((2, 2)), dma((2,)), dma, dma((8,)),
        dma, dma((2, 2)), dma((2,)), dma, dma((8,)),
        dma, dma, dma, dma, dma, dma,
        dma((2, 2, 8)), dma((2, 2, 8)),
        dma((2, NZ)), dma((2, NZ)), dma((3,)),
        dma((NZ,)), dma((NZ,)),
        dma, dma, dma, dma, dma, dma,
        dma, dma((NX, NC)),
        dma((2,)),
    ]
    return pl.pallas_call(
        kernel,
        out_shape=jax.ShapeDtypeStruct((NX, 64, NOUT), F32),
        in_specs=[
            pl.BlockSpec(memory_space=pl.ANY),
            pl.BlockSpec(memory_space=pl.ANY),
            pl.BlockSpec(memory_space=pl.ANY),
        ],
        out_specs=pl.BlockSpec(memory_space=pltpu.VMEM),
        scratch_shapes=scratch,
        compiler_params=pltpu.CompilerParams(
            collective_id=0, has_side_effects=True, vmem_limit_bytes=60 * 1024 * 1024
        ),
    )(activations, w, ow)


def solution(mesh):
    return jax.shard_map(
        shards,
        mesh=mesh,
        in_specs=(P(None, "row", "col"), P(None, None, "row", "col"), P("row", "col", None)),
        out_specs=P(None, "col", "row"),
        check_vma=False,
    )
```

time: 128 us -> 117 us (0.914)
  Pallas kernels: 125 us -> 115 us
    pallas_call x1, Pallas kernels: 125 us -> 115 us  [shards(): pl.pallas_call(kernel, out_shape=jax.ShapeDtypeStruct((NX, 64, NOUT), F32...]
where the time goes in v2:
time: 117 us
  Pallas kernels  115 us (98%)
  local copies, waits for them, and re-layouts  1.64 us (1%)
    pallas_call x1, Pallas kernels, shards(): pl.pallas_call(kernel, out_shape=jax.ShapeDtypeStruct((NX, 64, NOUT), F32...  115 us

profile of v2, /device:TPU:1, one launch (start us, length us, event | category | flops | bytes accessed | tf_op | source)
XLA Modules:
  0.0 116.7 jit_solution(726001105284504918)
XLA Ops:
  0.0 115.1 %shard_map.37 = f32[4,64,48]{2,1,0:T(8,128)} custom-call(f32[4,2,1536]{2,1,0:T(2,128)} %act.1, f32[1152,128]{1,0:T(8,128)} %bitcast.2, f32[384,128]{1,0:T(8,128)} %bitcast.3), custom_call_target="tpu_custom_call" | custom-call | tf_op jit(solution)/shard_map/pallas_call | solution.py:645
  115.1 1.6 %copy.4 = f32[4,64,48]{1,2,0:T(8,128)} copy(f32[4,64,48]{2,1,0:T(8,128)} %shard_map.37) | data formatting | bytes 98304 | tf_op jit(solution)/shard_map/pallas_call | solution.py:645

commit v3 on v2

--- a/solution.py
+++ b/solution.py
@@ -15,10 +15,12 @@
 LANE = 128
 TILES = 48
 KT = TILES // NX
-R1, R2 = 64, 32
+R = 2 * TILES
+RA = 48
+FAR = 5
 HEADS = 32
 NZZ = 8
-A1 = 80
+A1 = 64
 FEAT = 96
 NOUT = 48
 
@@ -29,9 +31,9 @@
 
 
 def kernel(act, w, ow, out, *scratch):
-    (chunk, g1, g2, wb, whl, ghl, ob, owhl, msg, rcv, kv, att, fs, fr, acc,
+    (chunk, g, wb, whl, ghl, ob, owhl, msg, rcv, kv, att, fs, fr, acc,
      act_s, act_r, w_s, w_r, wf_r, wc_s, wc_r, o_s, o_r, of_r, oc_s, oc_r,
-     z1_s, z2_s, y_s, h_s, c_s, p_s, r1, r2, ry, rh, rp, rc1, rc2,
+     z1_s, z2_s, y_s, h_s, c_s, p_s, r1, r2, ry, rh, rp, rc,
      a2a_s, a2a_r, kv_s, kv_r, b_s, b_r, f_s, f_r, loc) = scratch
     row = lax.axis_index("row")
     x = lax.axis_index("col")
@@ -66,20 +68,24 @@
     zp, zm = wrap(z + 1, NZ), wrap(z - 1, NZ)
 
     bar = pltpu.get_barrier_semaphore()
-
-    def greet(k, carry):
-        other = (me + k) % (NY * NZ)
-        pl.semaphore_signal(bar, inc=1, device_id=(other * 2 + c, x), device_id_type=MESH)
-        return carry
-
-    lax.fori_loop(1, NY * NZ, greet, 0)
     for dx in range(NX):
         for dc in range(NC):
             if dx or dc:
                 pl.semaphore_signal(
                     bar, inc=1, device_id=dev(y, z, (c + dc) % 2, (x + dx) % NX), device_id_type=MESH
                 )
-    pl.semaphore_wait(bar, NY * NZ - 1 + NX * NC - 1)
+
+    @pl.when(near)
+    def _():
+        for dz in (1, -1, FAR, -FAR):
+            pl.semaphore_signal(bar, inc=1, device_id=dev(y, wrap(z + dz, NZ), 1, x), device_id_type=MESH)
+        for yy in (yp, ym, yo):
+            pl.semaphore_signal(bar, inc=1, device_id=dev(yy, z, 1, x), device_id_type=MESH)
+        pl.semaphore_wait(bar, NX * NC - 1 + 4 + NY - 1)
+
+    @pl.when(far)
+    def _():
+        pl.semaphore_wait(bar, NX * NC - 1)
 
     for i in range(1, NX):
         xt = (x + i) % NX
@@ -186,36 +192,60 @@
     def back(d, s):
         return wrap(z - s, NZ) if d == 0 else wrap(z + s, NZ)
 
-    def z1(cls, d, s, half=False):
-        slot = back(d, s - 1)
-        piece = g1.at[y, slot, cls, pl.ds(d * (R1 // 2), R1 // 2)] if half else g1.at[y, slot, cls]
-        remote(piece, piece, z1_s, r1.at[cls, d, s - 1], dev(y, zp if d == 0 else zm, 1, x))
-
-    def z2(cls, d, s, half=False):
-        slot = back(d, s - 1)
-        piece = g2.at[:, slot, cls, pl.ds(d * (R2 // 2), R2 // 2)] if half else g2.at[:, slot, cls]
-        remote(piece, piece, z2_s, r2.at[cls, d, s - 1], dev(y, zp if d == 0 else zm, 1, x))
-
-    def y1(slot):
-        piece = g1.at[y, slot]
+    def onward(d, k):
+        return dev(y, wrap(z + k, NZ) if d == 0 else wrap(z - k, NZ), 1, x)
+
+    def z1(cls, d, s):
+        if s < FAR:
+            piece = g.at[y, back(d, s - 1), cls, pl.ds(0, RA)]
+        elif s == FAR:
+            piece = g.at[y, z, cls]
+        elif s < NZ // 2:
+            piece = g.at[y, back(d, s - 1), cls]
+        else:
+            piece = g.at[y, back(d, s - 1), cls, pl.ds(d * (R // 2), R // 2)]
+        remote(piece, piece, z1_s, r1.at[cls, d, s - 1], onward(d, FAR if s == FAR else 1))
+
+    def z1wait(cls, d, s):
+        if s < FAR:
+            piece = g.at[y, back(d, s), cls, pl.ds(0, RA)]
+        elif s < NZ // 2:
+            piece = g.at[y, back(d, s), cls]
+        else:
+            piece = g.at[y, back(d, s), cls, pl.ds(d * (R // 2), R // 2)]
+        wait(piece, r1.at[cls, d, s - 1])
+
+    def z2(cls, d, s):
+        piece = g.at[:, back(d, s - 1), cls, pl.ds(RA, R - RA)]
+        remote(piece, piece, z2_s, r2.at[cls, d, s - 1], onward(d, 1))
+
+    def y1(slot, n):
+        piece = g.at[y, slot, :, pl.ds(0, n)]
         remote(piece, piece, y_s, ry.at[0, slot], dev(yp, z, 1, x))
         remote(piece, piece, y_s, ry.at[1, slot], dev(ym, z, 1, x))
-        core(g1.at[y, slot, 0], rc1.at[slot])
-
-    def y1pass(slot):
-        wait(g1.at[ym, slot], ry.at[0, slot])
-        piece = g1.at[ym, slot, :, pl.ds(0, R1 // 2)]
+        core(g.at[y, slot, 0, pl.ds(0, n)], rc.at[slot])
+
+    def y1pass(slot, n):
+        wait(g.at[ym, slot, :, pl.ds(0, n)], ry.at[0, slot])
+        piece = g.at[ym, slot, :, pl.ds(0, n // 2)]
         remote(piece, piece, h_s, rh.at[0, slot], dev(yp, z, 1, x))
-        wait(g1.at[yp, slot], ry.at[1, slot])
-        piece = g1.at[yp, slot, :, pl.ds(R1 // 2, R1 // 2)]
+        wait(g.at[yp, slot, :, pl.ds(0, n)], ry.at[1, slot])
+        piece = g.at[yp, slot, :, pl.ds(n // 2, n // 2)]
         remote(piece, piece, h_s, rh.at[1, slot], dev(ym, z, 1, x))
-        core(g1.at[ym, slot, 0], rc1.at[slot])
-        core(g1.at[yp, slot, 0], rc1.at[slot])
-
-    def y1last(slot):
-        wait(g1.at[yo, slot, :, pl.ds(0, R1 // 2)], rh.at[0, slot])
-        wait(g1.at[yo, slot, :, pl.ds(R1 // 2, R1 // 2)], rh.at[1, slot])
-        core(g1.at[yo, slot, 0], rc1.at[slot])
+        core(g.at[ym, slot, 0, pl.ds(0, n)], rc.at[slot])
+        core(g.at[yp, slot, 0, pl.ds(0, n)], rc.at[slot])
+
+    def y1last(slot, n):
+        wait(g.at[yo, slot, :, pl.ds(0, n // 2)], rh.at[0, slot])
+        wait(g.at[yo, slot, :, pl.ds(n // 2, n // 2)], rh.at[1, slot])
+        core(g.at[yo, slot, 0, pl.ds(0, n)], rc.at[slot])
+
+    def both(s):
+        if s == 0:
+            return [(z, RA)]
+        if s == 4:
+            return [(back(0, 8), R)] + [(back(d, 4), RA) for d in range(2)]
+        return [(back(d, s + 4), R) for d in range(2)] + [(back(d, s), RA) for d in range(2)]
 
     @pl.when(near)
     def _():
@@ -234,61 +264,50 @@
             normed = (data - center) * scale
             for t in range(TILES):
                 v = normed[t // KT, :, t % KT * LANE : (t % KT + 1) * LANE]
-                if 2 * t < R1:
-                    g1[y, z, cls, pl.ds(2 * t, 2), :] = v
-                else:
-                    g2[y, z, cls, pl.ds(2 * t - R1, 2), :] = v
-        for cls in range(2):
-            for d in range(2):
-                z1(cls, d, 1)
-        own2 = g2.at[y, z]
+                g[y, z, cls, pl.ds(2 * t, 2), :] = v
+        for s in (FAR, 1):
+            for cls in range(2):
+                for d in range(2):
+                    z1(cls, d, s)
+        own2 = g.at[y, z, :, pl.ds(RA, R - RA)]
         for k, target in enumerate((yp, ym, yo)):
             remote(own2, own2, p_s, rp.at[k], dev(target, z, 1, x))
-        y1(z)
+        y1(z, RA)
         for k, origin in enumerate((ym, yp, yo)):
-            wait(g2.at[origin, z], rp.at[k])
+            wait(g.at[origin, z, :, pl.ds(RA, R - RA)], rp.at[k])
         for cls in range(2):
             for d in range(2):
                 z2(cls, d, 1)
-        core(g2.at[:, z, 0], rc2.at[z])
-        for s in range(1, 8):
-            half = s == 7
+        core(g.at[:, z, 0, pl.ds(RA, R - RA)], rc.at[z])
+        weights(1)
+        for s in range(1, 5):
+            for q in (s + 4, s):
+                for cls in range(2):
+                    for d in range(2):
+                        z1wait(cls, d, q)
+                        if s < 4:
+                            z1(cls, d, q + 1)
+            for slot, n in both(s):
+                y1(slot, n)
+            for slot, n in both(s - 1):
+                y1pass(slot, n)
             for cls in range(2):
                 for d in range(2):
-                    wait(g1.at[y, back(d, s), cls], r1.at[cls, d, s - 1])
-                    z1(cls, d, s + 1, half)
+                    wait(g.at[:, back(d, s), cls, pl.ds(RA, R - RA)], r2.at[cls, d, s - 1])
+                    if s < 4:
+                        z2(cls, d, s + 1)
             for d in range(2):
-                y1(back(d, s))
-            for cls in range(2):
-                for d in range(2):
-                    wait(g2.at[:, back(d, s), cls], r2.at[cls, d, s - 1])
-                    z2(cls, d, s + 1, half)
-            for d in range(2):
-                core(g2.at[:, back(d, s), 0], rc2.at[back(d, s)])
-            for d in range(1 if s == 1 else 2):
-                y1pass(back(d, s - 1))
+                core(g.at[:, back(d, s), 0, pl.ds(RA, R - RA)], rc.at[back(d, s)])
             if s > 1:
-                for d in range(1 if s == 2 else 2):
-                    y1last(back(d, s - 2))
-            weights(s)
-        opp = back(0, 8)
-        for cls in range(2):
-            for d in range(2):
-                wait(g1.at[y, opp, cls, pl.ds(d * (R1 // 2), R1 // 2)], r1.at[cls, d, 7])
-        y1(opp)
-        for d in range(2):
-            y1pass(back(d, 7))
-        for cls in range(2):
-            for d in range(2):
-                wait(g2.at[:, opp, cls, pl.ds(d * (R2 // 2), R2 // 2)], r2.at[cls, d, 7])
-        core(g2.at[:, opp, 0], rc2.at[opp])
-        y1pass(opp)
-        for d in range(2):
-            y1last(back(d, 6))
-        for d in range(2):
-            y1last(back(d, 7))
+                for slot, n in both(s - 2):
+                    y1last(slot, n)
+            for k in ((2, 3), (4,), (5, 6), (7,))[s - 1]:
+                weights(k)
+        for slot, n in both(4):
+            y1pass(slot, n)
+        for slot, n in both(3) + both(4):
+            y1last(slot, n)
         weights(8)
-        y1last(opp)
 
     @pl.when(far)
     def _():
@@ -296,20 +315,15 @@
             weights(s)
 
         def arrive(slot, carry):
-            wait(g1.at[:, slot, 0], rc1.at[slot])
-            wait(g2.at[:, slot, 0], rc2.at[slot])
+            wait(g.at[:, slot, 0], rc.at[slot])
             return carry
 
         lax.fori_loop(0, NZ, arrive, 0)
 
-    f1 = g1.reshape(NY * NZ * 2 * R1, LANE)
-    f2 = g2.reshape(NY * NZ * 2 * R2, LANE)
+    flat_g = g.reshape(NY * NZ * NC * R, LANE)
     for t in range(TILES):
         for b in range(2):
-            if 2 * t < R1:
-                v = f1[pl.ds(c * R1 + 2 * t + b, NY * NZ, stride=2 * R1), :]
-            else:
-                v = f2[pl.ds(c * R2 + 2 * t - R1 + b, NY * NZ, stride=2 * R2), :]
+            v = flat_g[pl.ds(c * R + 2 * t + b, NY * NZ, stride=NC * R), :]
             hi, lo = split(v)
             lanes = pl.ds(t % KT * LANE, LANE)
             ghl[t // KT, pl.ds(b * 64, 64), lanes] = hi
@@ -353,12 +367,12 @@
 
     @pl.when(near)
     def _():
-        drain(z1_s, 4 * (7 * R1 + R1 // 2))
-        drain(z2_s, 4 * NY * (7 * R2 + R2 // 2))
-        drain(y_s, NZ * 2 * 2 * R1)
-        drain(h_s, NZ * 2 * R1)
-        drain(c_s, NZ * NY * (R1 + R2))
-        drain(p_s, 3 * 2 * R2)
+        drain(z1_s, 4 * (4 * RA + 3 * R + R // 2))
+        drain(z2_s, 4 * 4 * NY * (R - RA))
+        drain(y_s, 4 * (9 * RA + 7 * R))
+        drain(h_s, 2 * (9 * RA + 7 * R))
+        drain(c_s, NZ * NY * R)
+        drain(p_s, 3 * 2 * (R - RA))
 
     gather_pass(ob, OH, 0, 1, *O)
     gather_pass(ob, OH, 1, 0, *O)
@@ -409,44 +423,59 @@
         for d2 in range(2):
             att[zz0, y, c, pl.ds(d2, 64, stride=2), :] = o[d2 * 64 : d2 * 64 + 64]
 
-    A2 = LANE - A1
-
-    def slot_of(d, k):
-        return wrap(zz0 - k, NZZ) if d == 0 else wrap((z + 1) // 2 + k, NZZ)
-
-    def b1(cls, d, k, half=False):
-        slot = slot_of(d, k)
-        rows = pl.ds(d * (A1 // 2), A1 // 2) if half else pl.ds(0, A1)
-        piece = att.at[slot, y, cls, rows]
-        remote(piece, piece, z1_s, r1.at[cls, d, k], dev(y, zp if d == 0 else zm, 1, x))
-
-    def b2(cls, d, k, half=False):
-        slot = slot_of(d, k)
-        rows = pl.ds(A1 + d * (A2 // 2), A2 // 2) if half else pl.ds(A1, A2)
-        piece = att.at[slot, :, cls, rows]
-        remote(piece, piece, z2_s, r2.at[cls, d, k], dev(y, zp if d == 0 else zm, 1, x))
-
-    def v1(slot, own=False):
-        piece = att.at[slot, y, :, pl.ds(0, A1)]
+    def slot_of(d, s):
+        return back(d, s) // 2
+
+    def b1(cls, d, s):
+        if s < FAR:
+            piece = att.at[slot_of(d, s - 1), y, cls, pl.ds(0, A1)]
+        elif s < NZ // 2:
+            piece = att.at[slot_of(d, s - 1 if s > FAR else 0), y, cls]
+        else:
+            piece = att.at[slot_of(d, s - 1), y, cls, pl.ds(d * (LANE // 2), LANE // 2)]
+        remote(piece, piece, z1_s, r1.at[cls, d, s - 1], onward(d, FAR if s == FAR else 1))
+
+    def b1wait(cls, d, s):
+        if s < FAR:
+            piece = att.at[slot_of(d, s), y, cls, pl.ds(0, A1)]
+        elif s < NZ // 2:
+            piece = att.at[slot_of(d, s), y, cls]
+        else:
+            piece = att.at[slot_of(d, s), y, cls, pl.ds(d * (LANE // 2), LANE // 2)]
+        wait(piece, r1.at[cls, d, s - 1])
+
+    def b2(cls, d, s):
+        piece = att.at[slot_of(d, s - 1), :, cls, pl.ds(A1, LANE - A1)]
+        remote(piece, piece, z2_s, r2.at[cls, d, s - 1], onward(d, 1))
+
+    def v1(slot, n, own=False):
+        piece = att.at[slot, y, :, pl.ds(0, n)]
         remote(piece, piece, y_s, ry.at[0, slot], dev(yp, z, 1, x))
         remote(piece, piece, y_s, ry.at[1, slot], dev(ym, z, 1, x))
         if not own:
-            core(att.at[slot, y, 0, pl.ds(0, A1)], rc1.at[slot])
-
-    def v1pass(slot):
-        wait(att.at[slot, ym, :, pl.ds(0, A1)], ry.at[0, slot])
-        piece = att.at[slot, ym, :, pl.ds(0, A1 // 2)]
+            core(att.at[slot, y, 0, pl.ds(0, n)], rc.at[slot])
+
+    def v1pass(slot, n):
+        wait(att.at[slot, ym, :, pl.ds(0, n)], ry.at[0, slot])
+        piece = att.at[slot, ym, :, pl.ds(0, n // 2)]
         remote(piece, piece, h_s, rh.at[0, slot], dev(yp, z, 1, x))
-        wait(att.at[slot, yp, :, pl.ds(0, A1)], ry.at[1, slot])
-        piece = att.at[slot, yp, :, pl.ds(A1 // 2, A1 // 2)]
+        wait(att.at[slot, yp, :, pl.ds(0, n)], ry.at[1, slot])
+        piece = att.at[slot, yp, :, pl.ds(n // 2, n // 2)]
         remote(piece, piece, h_s, rh.at[1, slot], dev(ym, z, 1, x))
-        core(att.at[slot, ym, 0, pl.ds(0, A1)], rc1.at[slot])
-        core(att.at[slot, yp, 0, pl.ds(0, A1)], rc1.at[slot])
-
-    def v1last(slot):
-        wait(att.at[slot, yo, :, pl.ds(0, A1 // 2)], rh.at[0, slot])
-        wait(att.at[slot, yo, :, pl.ds(A1 // 2, A1 // 2)], rh.at[1, slot])
-        core(att.at[slot, yo, 0, pl.ds(0, A1)], rc1.at[slot])
+        core(att.at[slot, ym, 0, pl.ds(0, n)], rc.at[slot])
+        core(att.at[slot, yp, 0, pl.ds(0, n)], rc.at[slot])
+
+    def v1last(slot, n):
+        wait(att.at[slot, yo, :, pl.ds(0, n // 2)], rh.at[0, slot])
+        wait(att.at[slot, yo, :, pl.ds(n // 2, n // 2)], rh.at[1, slot])
+        core(att.at[slot, yo, 0, pl.ds(0, n)], rc.at[slot])
+
+    def places(s):
+        if s == 0:
+            return [(zz0, A1)]
+        if s == 4:
+            return [(slot_of(0, 8), LANE)] + [(slot_of(d, 4), A1) for d in range(2)]
+        return [(slot_of(d, s + 4), LANE) for d in range(2)] + [(slot_of(d, s), A1) for d in range(2)]
 
     acc2 = acc.at[pl.ds(0, 4 * NOUT)]
     acc2[...] = jnp.zeros((4 * NOUT, 2 * LANE), F32)
@@ -456,96 +485,85 @@
         hi, lo = split(block)
         acc2[...] += jnp.dot(owhl[slot], jnp.concatenate([hi, lo], 1), preferred_element_type=F32)
 
-    def z1wait(k, n):
+    def round_of(s, before):
+        for q in (s + 4, s):
+            for cls in range(2):
+                for d in range(2):
+                    b1wait(cls, d, q)
+                    if s < 4:
+                        b1(cls, d, q + 1)
+        for slot, n in places(s):
+            v1(slot, n)
+        for slot, n in before:
+            v1pass(slot, n)
         for cls in range(2):
             for d in range(2):
-                wait(att.at[slot_of(d, k), y, cls, pl.ds(0, A1)], r1.at[cls, d, n])
-                b1(cls, d, k, n == 3)
+                wait(att.at[slot_of(d, s), :, cls, pl.ds(A1, LANE - A1)], r2.at[cls, d, s - 1])
+                if s < 4:
+                    b2(cls, d, s + 1)
         for d in range(2):
-            v1(slot_of(d, k))
-
-    def z2wait(k, n):
+            core(att.at[slot_of(d, s), :, 0, pl.ds(A1, LANE - A1)], rc.at[slot_of(d, s)])
+        for slot, n in before:
+            v1last(slot, n)
+        for slot, n in before:
+            finish(slot, 1)
+
+    def last_of(slots):
+        for slot, n in slots:
+            v1pass(slot, n)
+        for slot, n in slots:
+            v1last(slot, n)
+        for slot, n in slots:
+            finish(slot, 1)
+
+    @pl.when(near & even)
+    def _():
+        wait(att.at[zz0, y, 0], b_r)
+        for s in (FAR, 1):
+            for cls in range(2):
+                for d in range(2):
+                    b1(cls, d, s)
+        own = att.at[zz0, y, :, pl.ds(A1, LANE - A1)]
+        for k, target in enumerate((yp, ym, yo)):
+            remote(own, own, p_s, rp.at[k], dev(target, z, 1, x))
+        v1(zz0, A1, True)
+        for k, origin in enumerate((ym, yp, yo)):
+            wait(att.at[zz0, origin, :, pl.ds(A1, LANE - A1)], rp.at[k])
         for cls in range(2):
             for d in range(2):
-                wait(att.at[slot_of(d, k), :, cls, pl.ds(A1, A2)], r2.at[cls, d, n])
-                b2(cls, d, k, n == 3)
-        for d in range(2):
-            core(att.at[slot_of(d, k), :, 0, pl.ds(A1, A2)], rc2.at[slot_of(d, k)])
-
-    def lagged(slots):
-        for slot in slots:
-            v1pass(slot)
-        for slot in slots:
-            v1last(slot)
-        for slot in slots:
-            finish(slot, 1)
-
-    @pl.when(near & even)
-    def _():
-        wait(att.at[zz0, y, 0], b_r)
-        for cls in range(2):
-            for d in range(2):
-                b1(cls, d, 0)
-        own = att.at[zz0, y, :, pl.ds(A1, A2)]
-        for k, target in enumerate((yp, ym, yo)):
-            remote(own, own, p_s, rp.at[k], dev(target, z, 1, x))
-        v1(zz0, True)
-        for k, origin in enumerate((ym, yp, yo)):
-            wait(att.at[zz0, origin, :, pl.ds(A1, A2)], rp.at[k])
-        for cls in range(2):
-            for d in range(2):
-                b2(cls, d, 0)
+                b2(cls, d, 1)
         for origin in (ym, yp, yo):
-            core(att.at[zz0, origin, 0, pl.ds(A1, A2)], rc2.at[zz0])
-        for k in range(1, 4):
-            z1wait(k, k - 1)
-            z2wait(k, k - 1)
-            lagged([zz0] if k == 1 else [slot_of(0, k - 1), slot_of(1, k - 1)])
-        slot = slot_of(0, 4)
-        for cls in range(2):
-            for d in range(2):
-                wait(att.at[slot, y, cls, pl.ds(d * (A1 // 2), A1 // 2)], r1.at[cls, d, 3])
-        v1(slot)
-        for cls in range(2):
-            for d in range(2):
-                wait(att.at[slot, :, cls, pl.ds(A1 + d * (A2 // 2), A2 // 2)], r2.at[cls, d, 3])
-        core(att.at[slot, :, 0, pl.ds(A1, A2)], rc2.at[slot])
-        lagged([slot_of(0, 3), slot_of(1, 3)])
-        lagged([slot])
-        drain(p_s, 3 * 2 * A2)
+            core(att.at[zz0, origin, 0, pl.ds(A1, LANE - A1)], rc.at[zz0])
+        round_of(2, places(0))
+        round_of(4, places(2))
+        last_of(places(4))
 
     @pl.when(near & odd)
     def _():
-        for k in range(4):
-            z1wait(k, k)
-            z2wait(k, k)
-            if k:
-                lagged([slot_of(0, k - 1), slot_of(1, k - 1)])
-        lagged([slot_of(0, 3), slot_of(1, 3)])
+        round_of(1, [])
+        round_of(3, places(1))
+        last_of(places(3))
 
     def from_near(slot):
-        wait(att.at[slot, :, 0, pl.ds(0, A1)], rc1.at[slot])
-        wait(att.at[slot, :, 0, pl.ds(A1, A2)], rc2.at[slot])
+        wait(att.at[slot, :, 0], rc.at[slot])
         finish(slot, 0)
 
     @pl.when(far & even)
     def _():
         own = att.at[zz0, y, 0]
         remote(own, own, b_s, b_r, dev(y, z, 1, x))
-        wait(att.at[zz0, pl.ds(0, 3), 0, pl.ds(0, A1)], rc1.at[zz0])
-        wait(att.at[zz0, pl.ds(0, 3), 0, pl.ds(A1, A2)], rc2.at[zz0])
+        wait(att.at[zz0, pl.ds(0, 3), 0], rc.at[zz0])
         finish(zz0, 0)
-        for k in range(1, 4):
-            for d in range(2):
-                from_near(slot_of(d, k))
-        from_near(slot_of(0, 4))
+        for s in (2, 4):
+            for slot, n in places(s):
+                from_near(slot)
         wait(own, b_s)
 
     @pl.when(far & odd)
     def _():
-        for k in range(4):
-            for d in range(2):
-                from_near(slot_of(d, k))
+        for s in (1, 3):
+            for slot, n in places(s):
+                from_near(slot)
 
     sums = acc2[...]
     sums = sums[:, :LANE] + sums[:, LANE:]
@@ -592,21 +610,21 @@
     def _():
         wait(chunk.at[0, 0], act_s.at[0])
 
-    @pl.when(near)
-    def _():
-        drain(y_s, NZZ * 2 * 2 * A1)
-        drain(h_s, NZZ * 2 * A1)
-
     @pl.when(near & even)
     def _():
-        drain(z1_s, 16 * A1)
-        drain(z2_s, 16 * NY * A2)
+        drain(z1_s, 8 * A1 + 8 * LANE)
+        drain(z2_s, 8 * NY * (LANE - A1))
+        drain(y_s, 4 * (5 * A1 + 3 * LANE))
+        drain(h_s, 2 * (5 * A1 + 3 * LANE))
         drain(c_s, NZZ * NY * LANE - LANE)
+        drain(p_s, 3 * 2 * (LANE - A1))
 
     @pl.when(near & odd)
     def _():
-        drain(z1_s, 14 * A1)
-        drain(z2_s, 14 * NY * A2)
+        drain(z1_s, 8 * A1 + 6 * LANE)
+        drain(z2_s, 8 * NY * (LANE - A1))
+        drain(y_s, 4 * (4 * A1 + 4 * LANE))
+        drain(h_s, 2 * (4 * A1 + 4 * LANE))
         drain(c_s, NZZ * NY * LANE)
 
 
@@ -617,8 +635,7 @@
     vm = pltpu.VMEM
     scratch = [
         vm((NC, NX, 2, KT * LANE), F32),
-        vm((NY, NZ, NC, R1, LANE), F32),
-        vm((NY, NZ, NC, R2, LANE), F32),
+        vm((NY, NZ, NC, R, LANE), F32),
         vm((NC, NX, FEAT * KT, LANE), F32),
         vm((NX, 4 * FEAT, KT * LANE), BF16),
         vm((NX, 2 * LANE, KT * LANE), BF16),
@@ -635,9 +652,9 @@
         dma, dma((2, 2)), dma((2,)), dma, dma((8,)),
         dma, dma((2, 2)), dma((2,)), dma, dma((8,)),
         dma, dma, dma, dma, dma, dma,
-        dma((2, 2, 8)), dma((2, 2, 8)),
+        dma((2, 2, 8)), dma((2, 2, 4)),
         dma((2, NZ)), dma((2, NZ)), dma((3,)),
-        dma((NZ,)), dma((NZ,)),
+        dma((NZ,)),
         dma, dma, dma, dma, dma, dma,
         dma, dma((NX, NC)),
         dma((2,)),

time: 117 us -> 109 us (0.932)
  Pallas kernels: 115 us -> 107 us
    pallas_call x1, Pallas kernels: 115 us -> 107 us  [shards(): pl.pallas_call(kernel, out_shape=jax.ShapeDtypeStruct((NX, 64, NOUT), F32...]
where the time goes in v3:
time: 109 us; the launch traced here: 108 us
  Pallas kernels  107 us (98%)
  local copies, waits for them, and re-layouts  1.64 us (2%)
    pallas_call x1, Pallas kernels, shards(): pl.pallas_call(kernel, out_shape=jax.ShapeDtypeStruct((NX, 64, NOUT), F32...  107 us

profile of v3, /device:TPU:1, one launch (start us, length us, event | category | flops | bytes accessed | tf_op | source)
XLA Modules:
  0.0 108.4 jit_solution(6611647868878212988)
XLA Ops:
  0.0 106.8 %shard_map.37 = f32[4,64,48]{2,1,0:T(8,128)} custom-call(f32[4,2,1536]{2,1,0:T(2,128)} %act.1, f32[1152,128]{1,0:T(8,128)} %bitcast.2, f32[384,128]{1,0:T(8,128)} %bitcast.3), custom_call_target="tpu_custom_call" | custom-call | tf_op jit(solution)/shard_map/pallas_call | solution.py:662
  106.8 1.6 %copy.4 = f32[4,64,48]{1,2,0:T(8,128)} copy(f32[4,64,48]{2,1,0:T(8,128)} %shard_map.37) | data formatting | bytes 98304 | tf_op jit(solution)/shard_map/pallas_call | solution.py:662

commit v4 on v0

v4 whole, which is shorter than its diff:
```python
import jax
import jax.numpy as jnp
from jax import lax
from jax.experimental import pallas as pl
from jax.experimental.pallas import tpu as pltpu
from jax.sharding import PartitionSpec as P

MESH = pl.DeviceIdType.MESH
EPS = 1e-06
HIGHEST = lax.Precision.HIGHEST
F32 = jnp.float32
BF16 = jnp.bfloat16

NX, NY, NZ, NC = 4, 4, 16, 2
LANE = 128
TILES = 48
KT = TILES // NX
R = 2 * TILES
R1, R2 = 64, 32
STRAIGHT = 7
STREAMS = 4
HEADS = 32
NZZ = 8
A1 = 80
FEAT = 96
NOUT = 48


def split(x):
    hi = x.astype(BF16)
    return hi, (x - hi.astype(F32)).astype(BF16)


def kernel(act, w, ow, out, *scratch):
    (chunk, g, wb, whl, ghl, ob, owhl, msg, rcv, kv, att, fs, fr, turn, acc,
     act_s, act_r, w_s, w_r, wf_r, wn_s, wn_r, o_s, o_r, of_r, on_s, on_r,
     z1_s, z2_s, y_s, h_s, c_s, c2_s, p_s, r1, r2, ry, rh, rp, rc,
     a2a_s, a2a_r, kv_s, kv_r, b_s, b_r, f_s, f_r, loc) = scratch
    row = lax.axis_index("row")
    x = lax.axis_index("col")
    c = row % 2
    z = row // 2 % NZ
    y = row // (2 * NZ)
    me = y * NZ + z
    near, far = c == 1, c == 0
    even, odd = z % 2 == 0, z % 2 == 1
    zz0 = z // 2

    def dev(yy, zz, cc, xx):
        return ((yy * NZ + zz) * 2 + cc, xx)

    def wrap(v, n):
        return (v + n) % n

    def remote(src, dst, ssem, rsem, where):
        pltpu.make_async_remote_copy(
            src_ref=src, dst_ref=dst, send_sem=ssem, recv_sem=rsem, device_id=where, device_id_type=MESH
        ).start()

    def wait(ref, sem):
        pltpu.make_async_copy(ref, ref, sem).wait()

    flat = wb.reshape(NC * NX * FEAT * KT, LANE)

    def drain(sem, rows):
        wait(flat.at[pl.ds(0, rows)], sem)

    xp, xm, xo = wrap(x + 1, NX), wrap(x - 1, NX), wrap(x + 2, NX)
    yp, ym, yo = wrap(y + 1, NY), wrap(y - 1, NY), wrap(y + 2, NY)

    bar = pltpu.get_barrier_semaphore()

    def greet(where):
        pl.semaphore_signal(bar, inc=1, device_id=where, device_id_type=MESH)

    @pl.when(near)
    def _():
        greet(dev(y, z, 0, x))
        for i in range(1, NX):
            for cc in range(NC):
                greet(dev(y, z, cc, wrap(x + i, NX)))
        for dz in (1, -1):
            greet(dev(y, wrap(z + dz, NZ), 1, x))
        for yy in (yp, ym, yo):
            greet(dev(yy, z, 1, x))
        pl.semaphore_wait(bar, 1 + NX - 1 + 2 + NY - 1)

    @pl.when(far)
    def _():
        greet(dev(y, z, 1, x))
        for xx in (xp, xm):
            greet(dev(y, z, 0, xx))
        pl.semaphore_wait(bar, NX + 2)

    for i in range(1, NX):
        xt = (x + i) % NX
        remote(act.at[xt], chunk.at[c, x], act_s.at[i], act_r.at[c, i], dev(y, z, 1, xt))

    @pl.when(far)
    def _():
        remote(act.at[x], chunk.at[0, x], act_s.at[0], act_r.at[0, 0], dev(y, z, 1, x))

    @pl.when(near)
    def _():
        pltpu.make_async_copy(act.at[x], chunk.at[1, x], act_r.at[1, 0]).start()
        remote(w, wb.at[1, x], wn_s, wn_r, dev(y, z, 0, x))
        remote(ow, ob.at[1, x], on_s, on_r, dev(y, z, 0, x))

    def gather_send(src, buf, d2, half, ss, rs):
        for q, (first, target) in enumerate(((0, xp), (1, xm))):
            for p in (first, 1 - first):
                rows = pl.ds(p * half, half)
                remote(src.at[rows], buf.at[d2, x, rows], ss, rs.at[d2, q, p], dev(y, z, 0, target))

    def gather_pass(buf, d2, half, q, p, ss, rs, fr_):
        origin = xm if q == 0 else xp
        piece = buf.at[d2, origin, pl.ds(p * half, half)]
        wait(piece, rs.at[d2, q, p])
        if p == q:
            remote(piece, piece, ss, fr_.at[d2, q], dev(y, z, 0, xp if q == 0 else xm))

    def gather_last(buf, d2, half, q, fr_):
        wait(buf.at[d2, xo, pl.ds(q * half, half)], fr_.at[d2, q])

    WH = FEAT * KT // 2
    OH = NOUT * 8 // 2

    def wconv(d2, origin, p):
        def body(kt, carry):
            v = wb[d2, origin, pl.ds(p * WH + kt, FEAT // 2, stride=KT), :]
            hi, lo = split(v)
            lanes = pl.ds(pl.multiple_of(kt * LANE, LANE), LANE)
            at = d2 * FEAT + p * (FEAT // 2)
            whl[origin, pl.ds(at, FEAT // 2), lanes] = hi
            whl[origin, pl.ds(at + 2 * FEAT, FEAT // 2), lanes] = lo
            return carry

        lax.fori_loop(0, KT, body, 0)

    def core(piece, sem, sent):
        remote(piece, piece, sent, sem, dev(y, z, 0, x))

    def back(d, s):
        return wrap(z - s, NZ) if d == 0 else wrap(z + s, NZ)

    def onward(d, k):
        return dev(y, wrap(z + k, NZ) if d == 0 else wrap(z - k, NZ), 1, x)

    ONES = pl.ds(0, R1)
    TWOS = pl.ds(R1, R2)

    def cutting(d, s, first, n):
        if s < NZ // 2:
            return pl.ds(first, n)
        share = (n // 2 + 7) // 8 * 8
        return pl.ds(first + share, n - share) if d else pl.ds(first, share)

    def z1piece(u, d, s, t):
        n = R1 // 2
        return g.at[back(d, s - t), y, u // 2, cutting(d, s, u % 2 * n, n)]

    def z2piece(u, d, s, t):
        return g.at[back(d, s - t), pl.ds(u % 2 * 2, 2), u // 2, cutting(d, s, R1, R2)]

    def z1(u, d, s):
        piece = z1piece(u, d, s, 1)
        remote(piece, piece, z1_s, r1.at[u, d, s - 1], onward(d, 1))

    def z2(u, d, s):
        piece = z2piece(u, d, s, 1)
        remote(piece, piece, z2_s, r2.at[u, d, s - 1], onward(d, 1))

    def y1(slot, straight):
        piece = g.at[slot, y, :, ONES]
        remote(piece, piece, y_s, ry.at[0, slot], dev(yp, z, 1, x))
        remote(piece, piece, y_s, ry.at[1, slot], dev(ym, z, 1, x))
        if straight:
            remote(piece, piece, y_s, rh.at[0, slot], dev(yo, z, 1, x))
        core(piece, rc.at[slot], c_s)

    def y1pass(slot, straight):
        for q, origin, target in ((0, ym, yp), (1, yp, ym)):
            wait(g.at[slot, origin, :, ONES], ry.at[q, slot])
            if not straight:
                piece = g.at[slot, origin, :, pl.ds(q * (R1 // 2), R1 // 2)]
                remote(piece, piece, h_s, rh.at[q, slot], dev(target, z, 1, x))
        core(g.at[slot, ym, :, ONES], rc.at[slot], c_s)
        core(g.at[slot, yp, :, ONES], rc.at[slot], c_s)

    def y1last(slot, straight):
        if straight:
            wait(g.at[slot, yo, :, ONES], rh.at[0, slot])
        else:
            for q in range(2):
                wait(g.at[slot, yo, :, pl.ds(q * (R1 // 2), R1 // 2)], rh.at[q, slot])
        core(g.at[slot, yo, :, ONES], rc.at[slot], c_s)

    def spots(s):
        if s in (0, NZ // 2):
            return [(back(0, s), s >= STRAIGHT)]
        return [(back(d, s), s >= STRAIGHT) for d in range(2)]

    @pl.when(near)
    def _():
        for cls in range(2):
            for i in range(NX):
                wait(chunk.at[0, 0], act_r.at[cls, i])
        for cls in range(2):
            data = chunk[cls]
            width = TILES * LANE

            def mean(v):
                return jnp.sum(jnp.sum(v, 0, keepdims=True), 2, keepdims=True) / width

            center = mean(data)
            scale = lax.rsqrt(mean(data * data) - center * center + EPS)
            normed = (data - center) * scale
            for t in range(TILES):
                v = normed[t // KT, :, t % KT * LANE : (t % KT + 1) * LANE]
                g[z, y, cls, pl.ds(2 * t, 2), :] = v
            for u in (2 * cls, 2 * cls + 1):
                for d in range(2):
                    z1(u, d, 1)
        own2 = g.at[z, y, :, TWOS]
        for k, target in enumerate((yp, ym, yo)):
            remote(own2, own2, p_s, rp.at[k], dev(target, z, 1, x))
        y1(z, False)
        for k, origin in enumerate((ym, yp, yo)):
            wait(g.at[z, origin, :, TWOS], rp.at[k])
        for u in range(STREAMS):
            for d in range(2):
                z2(u, d, 1)
        core(g.at[z, :, :, TWOS], rc.at[z], c2_s)
        last = NZ // 2
        for s in range(1, last + 4):
            if s <= last:
                for u in range(STREAMS):
                    for d in range(2):
                        wait(z1piece(u, d, s, 0), r1.at[u, d, s - 1])
                        if s < last:
                            z1(u, d, s + 1)
                for spot in spots(s):
                    y1(*spot)
            t = s - 1
            if 1 <= t <= last:
                for u in range(STREAMS):
                    for d in range(2):
                        wait(z2piece(u, d, t, 0), r2.at[u, d, t - 1])
                        if t < last:
                            z2(u, d, t + 1)
                for slot, _ in spots(t):
                    core(g.at[slot, :, :, TWOS], rc.at[slot], c2_s)
            if 0 <= s - 2 <= last:
                for spot in spots(s - 2):
                    y1pass(*spot)
            if 0 <= s - 3 <= last:
                for spot in spots(s - 3):
                    y1last(*spot)

    @pl.when(far)
    def _():
        own = pltpu.make_async_copy(w, wb.at[0, x], loc.at[0])
        own.start()
        gather_send(w, wb, 0, WH, w_s, w_r)
        wait(wb.at[1, x], wn_r)
        gather_send(wb.at[1, x], wb, 1, WH, w_s, w_r)
        own.wait()
        for d2 in range(2):
            for p in range(2):
                wconv(d2, x, p)
        for p in range(2):
            for d2 in range(2):
                gather_pass(wb, d2, WH, 0, p, w_s, w_r, wf_r)
                gather_pass(wb, d2, WH, 1, 1 - p, w_s, w_r, wf_r)
            for d2 in range(2):
                wconv(d2, xm, p)
                wconv(d2, xp, 1 - p)
        own = pltpu.make_async_copy(ow, ob.at[0, x], loc.at[1])
        own.start()
        gather_send(ow, ob, 0, OH, o_s, o_r)
        wait(ob.at[1, x], on_r)
        gather_send(ob.at[1, x], ob, 1, OH, o_s, o_r)
        for d2 in range(2):
            for q in range(2):
                gather_last(wb, d2, WH, q, wf_r)
                wconv(d2, xo, q)
        own.wait()

        flat_g = g.reshape(NZ * NY * NC * R, LANE)

        def arrive(k, carry):
            away = (k + 1) // 2
            slot = wrap(z + away - 2 * away * (k % 2), NZ)
            wait(g.at[slot], rc.at[slot])
            rows = pl.ds(pl.multiple_of(slot * 16, 16), 16)
            low = pl.ds(pl.multiple_of(2 * LANE + slot * 16, 16), 16)
            for t in range(TILES):
                v = jnp.concatenate(
                    [flat_g[pl.ds(slot * (NY * NC * R) + 2 * t + b, NY * NC, stride=R), :] for b in range(2)], 0
                )
                hi, lo = split(v)
                lanes = pl.ds(t % KT * LANE, LANE)
                ghl[t // KT, rows, lanes] = hi
                ghl[t // KT, low, lanes] = lo
            return carry

        lax.fori_loop(0, NZ, arrive, 0)

        acc[...] = jnp.zeros_like(acc)
        turned = (((1,), (1,)), ((), ()))

        def project(k, carry):
            acc[...] += lax.dot_general(whl[k, : 2 * FEAT], ghl[k], turned, preferred_element_type=F32)
            acc[:, :256] += lax.dot_general(
                whl[k, 2 * FEAT :], ghl[k, :256], turned, preferred_element_type=F32
            )
            return carry

        lax.fori_loop(0, NX, project, 0)
        triples = acc[:, :256] + acc[:, 256:]

        msg[...] = jnp.zeros_like(msg)
        for cls in range(2):
            for d2 in range(2):
                for s in range(3):
                    at = d2 * FEAT + s * HEADS
                    msg[cls, pl.ds(2 * s + d2, HEADS, stride=8), :] = triples[
                        at : at + HEADS, cls * LANE : (cls + 1) * LANE
                    ]

        def post(k, carry):
            h = (k + me // 2) % HEADS
            there = h // NZZ * NZ + h % NZZ * 2
            rows = pl.ds(pl.multiple_of(h * 8, 8), 8)
            dst = rcv.at[pl.ds(pl.multiple_of(me * 8, 8), 8)]
            remote(msg.at[1, rows], dst, a2a_s, a2a_r, (there * 2 + 1, x))

            @pl.when(there != me)
            def _():
                remote(msg.at[0, rows], dst, a2a_s, a2a_r, (there * 2, x))

            @pl.when(there == me)
            def _():
                pltpu.make_async_copy(msg.at[0, rows], dst, a2a_r).start()

            return carry

        lax.fori_loop(0, HEADS, post, 0)

        for p in range(2):
            for d2 in range(2):
                gather_pass(ob, d2, OH, 0, p, o_s, o_r, of_r)
                gather_pass(ob, d2, OH, 1, 1 - p, o_s, o_r, of_r)
        for d2 in range(2):
            for q in range(2):
                gather_last(ob, d2, OH, q, of_r)

        for d2 in range(2):
            for hq in range(NX):
                for j in range(8):
                    hi, lo = split(ob[d2, hq, pl.ds(j, NOUT, stride=8), :])
                    lanes = pl.ds(hq * LANE, LANE)
                    owhl[j, pl.ds(d2 * NOUT, NOUT), lanes] = hi
                    owhl[j, pl.ds(2 * NOUT + d2 * NOUT, NOUT), lanes] = lo

    @pl.when(near)
    def _():
        drain(z1_s, 4 * (7 * R1 + R1 // 2))
        drain(z2_s, 4 * NY * (7 * R2 + R2 // 2))
        straight = 2 * (NZ // 2 - STRAIGHT) + 1
        drain(y_s, (NZ * 2 + straight) * 2 * R1)
        drain(h_s, (NZ - straight) * 2 * R1)
        drain(c_s, NZ * NY * NC * R1)
        drain(c2_s, NZ * NY * NC * R2)
        drain(p_s, 3 * 2 * R2)

    def norm_rows(v):
        m = jnp.sum(v, 0, keepdims=True) / LANE
        q = jnp.sum(v * v, 0, keepdims=True) / LANE - m * m
        return (v - m) * lax.rsqrt(q + EPS)

    @pl.when(even)
    def _():
        wait(rcv, a2a_r)

        def third(s):
            return jnp.concatenate([rcv[pl.ds(2 * s + d2, 64, stride=8), :] for d2 in range(2)], 0)

        kv[c, pl.ds(0, LANE)] = norm_rows(third(1))
        kv[c, pl.ds(LANE, LANE)] = third(2)
        mine = kv.at[c]
        remote(mine, mine, kv_s, kv_r, dev(y, z, 1 - c, x))
        queries = norm_rows(third(0)) * (LANE ** -0.5)
        wait(kv.at[1 - c], kv_r)
        es = []
        for k in range(2):
            keys = kv[k, pl.ds(0, LANE)].T
            es.append(jnp.exp(jnp.dot(keys, queries, precision=HIGHEST, preferred_element_type=F32)))
        norm = jnp.sum(es[0], 0, keepdims=True) + jnp.sum(es[1], 0, keepdims=True)
        o = sum(
            jnp.dot(kv[k, pl.ds(LANE, LANE)], es[k] / norm, precision=HIGHEST, preferred_element_type=F32)
            for k in range(2)
        )
        for d2 in range(2):
            att[zz0, y, c, pl.ds(d2, 64, stride=2), :] = o[d2 * 64 : d2 * 64 + 64]

    def slot_of(d, s):
        return back(d, s) // 2

    def b1piece(u, d, s, t):
        n = A1 // 2
        return att.at[slot_of(d, s - t), y, u // 2, cutting(d, s, u % 2 * n, n)]

    def b2piece(u, d, s, t):
        return att.at[slot_of(d, s - t), pl.ds(u % 2 * 2, 2), u // 2, cutting(d, s, A1, LANE - A1)]

    def b1(u, d, s):
        piece = b1piece(u, d, s, 1)
        remote(piece, piece, z1_s, r1.at[u, d, s - 1], onward(d, 1))

    def b2(u, d, s):
        piece = b2piece(u, d, s, 1)
        remote(piece, piece, z2_s, r2.at[u, d, s - 1], onward(d, 1))

    FIRST = pl.ds(0, A1)
    SECOND = pl.ds(A1, LANE - A1)

    def v1(slot, straight, own=False):
        piece = att.at[slot, y, :, FIRST]
        remote(piece, piece, y_s, ry.at[0, slot], dev(yp, z, 1, x))
        remote(piece, piece, y_s, ry.at[1, slot], dev(ym, z, 1, x))
        if straight:
            remote(piece, piece, y_s, rh.at[0, slot], dev(yo, z, 1, x))
        if not own:
            core(piece, rc.at[slot], c_s)

    def v1pass(slot, straight):
        for q, origin, target in ((0, ym, yp), (1, yp, ym)):
            wait(att.at[slot, origin, :, FIRST], ry.at[q, slot])
            if not straight:
                piece = att.at[slot, origin, :, pl.ds(q * (A1 // 2), A1 // 2)]
                remote(piece, piece, h_s, rh.at[q, slot], dev(target, z, 1, x))
        core(att.at[slot, ym, :, FIRST], rc.at[slot], c_s)
        core(att.at[slot, yp, :, FIRST], rc.at[slot], c_s)

    def v1last(slot, straight):
        if straight:
            wait(att.at[slot, yo, :, FIRST], rh.at[0, slot])
        else:
            for q in range(2):
                wait(att.at[slot, yo, :, pl.ds(q * (A1 // 2), A1 // 2)], rh.at[q, slot])
        core(att.at[slot, yo, :, FIRST], rc.at[slot], c_s)

    def places(s):
        if s in (0, NZ // 2):
            return [(slot_of(0, s), s >= STRAIGHT)]
        return [(slot_of(d, s), s >= STRAIGHT) for d in range(2)]

    ACROSS = pl.ds(0, 2 * NOUT)

    @pl.when(far)
    def _():
        acc[ACROSS] = jnp.zeros((2 * NOUT, 4 * LANE), F32)

    def finish(slot):
        halves = [split(att[slot, :, cls].reshape(NY * LANE, LANE)) for cls in range(2)]
        hi = jnp.concatenate([h for h, _ in halves], 1)
        lo = jnp.concatenate([l for _, l in halves], 1)
        acc[ACROSS] += jnp.dot(
            owhl[slot, : 2 * NOUT], jnp.concatenate([hi, lo], 1), preferred_element_type=F32
        )
        acc[ACROSS, : 2 * LANE] += jnp.dot(owhl[slot, 2 * NOUT :], hi, preferred_element_type=F32)

    def round_of(s, before, earlier):
        last = NZ // 2
        for u in range(STREAMS):
            for d in range(2):
                wait(b1piece(u, d, s, 0), r1.at[u, d, s - 1])
                if s < last:
                    b1(u, d, s + 1)
        for place in places(s):
            v1(*place)
        for place in before:
            v1pass(*place)
        for u in range(STREAMS):
            for d in range(2):
                wait(b2piece(u, d, s, 0), r2.at[u, d, s - 1])
                if s < last:
                    b2(u, d, s + 1)
        for slot, _ in places(s):
            core(att.at[slot, :, :, SECOND], rc.at[slot], c_s)
        for place in earlier:
            v1last(*place)

    def last_of(before, earlier):
        for place in before:
            v1pass(*place)
        for place in earlier:
            v1last(*place)

    @pl.when(near & even)
    def _():
        core(att.at[zz0, y, 1], rc.at[zz0], c_s)
        wait(att.at[zz0, y, 0], b_r)
        for u in range(STREAMS):
            for d in range(2):
                b1(u, d, 1)
        own = att.at[zz0, y, :, SECOND]
        for k, target in enumerate((yp, ym, yo)):
            remote(own, own, p_s, rp.at[k], dev(target, z, 1, x))
        v1(zz0, False, True)
        for k, origin in enumerate((ym, yp, yo)):
            wait(att.at[zz0, origin, :, SECOND], rp.at[k])
        for u in range(STREAMS):
            for d in range(2):
                b2(u, d, 1)
        for origin in (ym, yp, yo):
            core(att.at[zz0, origin, :, SECOND], rc.at[zz0], c_s)
        round_of(2, places(0), [])
        round_of(4, places(2), places(0))
        round_of(6, places(4), places(2))
        round_of(8, places(6), places(4))
        last_of(places(8), places(6) + places(8))

    @pl.when(near & odd)
    def _():
        round_of(1, [], [])
        round_of(3, places(1), [])
        round_of(5, places(3), places(1))
        round_of(7, places(5), places(3))
        last_of(places(7), places(5) + places(7))

    def from_near(slot):
        wait(att.at[slot], rc.at[slot])
        finish(slot)

    @pl.when(far & even)
    def _():
        own = att.at[zz0, y, 0]
        remote(own, own, b_s, b_r, dev(y, z, 1, x))
        drain(rc.at[zz0], (2 * NY - 1) * LANE)
        finish(zz0)
        for s in (2, 4, 6, 8):
            for slot, _ in places(s):
                from_near(slot)
        wait(own, b_s)

    @pl.when(far & odd)
    def _():
        for s in (1, 3, 5, 7):
            for slot, _ in places(s):
                from_near(slot)

    @pl.when(far)
    def _():
        sums = acc[ACROSS, : 2 * LANE] + acc[ACROSS, 2 * LANE :]
        for k in range(2):
            mine = sums[:, k * LANE : (k + 1) * LANE]
            turn[pl.ds(k * LANE, LANE)] = jnp.concatenate([mine, jnp.zeros((LANE - 2 * NOUT, LANE), F32)], 0).T
        for q in range(NX):
            for cls in range(NC):
                mine = turn[pl.ds(q * NC + cls, 2 * NZ, stride=NY * NC), :]
                for cc in range(NC):
                    fs[q, cc, pl.ds(cls * 32, 32), pl.ds(0, NOUT)] = mine[:, cc * NOUT : cc * NOUT + NOUT]
        for dx in (2, 1, 3, 0):
            for cc in range(NC):
                if dx or cc:
                    tx = (x + dx) % NX
                    remote(fs.at[tx, cc], fr.at[x], f_s, f_r.at[dx], dev(y, z, cc, tx))
        fr[x] = fs[x, 0]

    @pl.when(near)
    def _():
        wait(fr.at[0], f_r.at[0])

    for dx in range(1, NX):
        wait(fr.at[0], f_r.at[dx])
    for i in range(NX):
        for cls in range(NC):
            for b in range(2):
                out[i, pl.ds(2 * cls + b, 16, stride=4), :] = fr[i, pl.ds(cls * 32 + b, 16, stride=2), :][:, :NOUT]

    for i in range(1, NX):
        wait(chunk.at[0, 0], act_s.at[i])

    @pl.when(even)
    def _():
        wait(kv.at[0], kv_s)

    @pl.when(far)
    def _():
        wait(chunk.at[0, 0], act_s.at[0])
        drain(w_s, 12 * WH)
        drain(o_s, 12 * OH)
        drain(f_s, 7 * 64)

    @pl.when(far & even)
    def _():
        drain(a2a_s, (2 * HEADS - 1) * 8)

    @pl.when(far & odd)
    def _():
        drain(a2a_s, 2 * HEADS * 8)

    @pl.when(near)
    def _():
        drain(wn_s, 2 * WH)
        drain(on_s, 2 * OH)

    @pl.when(near & even)
    def _():
        drain(z1_s, 2 * NC * 4 * A1)
        drain(z2_s, 2 * NC * 4 * NY * (LANE - A1))
        drain(y_s, (NZZ * 2 + 1) * 2 * A1)
        drain(h_s, (NZZ - 1) * 2 * A1)
        drain(c_s, NZZ * NY * NC * LANE - LANE)
        drain(p_s, 3 * 2 * (LANE - A1))

    @pl.when(near & odd)
    def _():
        up, down = 24, 16
        drain(z1_s, NC * (2 * 3 * A1 + 2 * up + 2 * down))
        drain(z2_s, NC * 7 * NY * (LANE - A1))
        drain(y_s, (NZZ * 2 + 2) * 2 * A1)
        drain(h_s, (NZZ - 2) * 2 * A1)
        drain(c_s, NZZ * NY * NC * LANE)


def shards(activations, input_weight, output_weight):
    w = input_weight.reshape(FEAT * KT, LANE)
    ow = output_weight.reshape(NOUT * 8, LANE)
    dma = pltpu.SemaphoreType.DMA
    vm = pltpu.VMEM
    scratch = [
        vm((NC, NX, 2, KT * LANE), F32),
        vm((NZ, NY, NC, R, LANE), F32),
        vm((NC, NX, FEAT * KT, LANE), F32),
        vm((NX, 4 * FEAT, KT * LANE), BF16),
        vm((NX, 4 * LANE, KT * LANE), BF16),
        vm((NC, NX, NOUT * 8, LANE), F32),
        vm((NZZ, 4 * NOUT, NY * LANE), BF16),
        vm((NC, HEADS * 8, LANE), F32),
        vm((NY * NZ * 8, LANE), F32),
        vm((NC, 2 * LANE, LANE), F32),
        vm((NZZ, NY, NC, LANE, LANE), F32),
        vm((NX, NC, 64, LANE), F32),
        vm((NX, 64, LANE), F32),
        vm((2 * LANE, LANE), F32),
        vm((2 * FEAT, 4 * LANE), F32),
        dma((NX,)), dma((NC, NX)),
        dma, dma((2, 2, 2)), dma((2, 2)), dma, dma,
        dma, dma((2, 2, 2)), dma((2, 2)), dma, dma,
        dma, dma, dma, dma, dma, dma, dma,
        dma((STREAMS, 2, 8)), dma((STREAMS, 2, 8)),
        dma((2, NZ)), dma((2, NZ)), dma((3,)),
        dma((NZ,)),
        dma, dma, dma, dma, dma, dma,
        dma, dma((NX,)),
        dma((2,)),
    ]
    return pl.pallas_call(
        kernel,
        out_shape=jax.ShapeDtypeStruct((NX, 64, NOUT), F32),
        in_specs=[
            pl.BlockSpec(memory_space=pl.ANY),
            pl.BlockSpec(memory_space=pl.ANY),
            pl.BlockSpec(memory_space=pl.ANY),
        ],
        out_specs=pl.BlockSpec(memory_space=pltpu.VMEM),
        scratch_shapes=scratch,
        compiler_params=pltpu.CompilerParams(
            collective_id=0, has_side_effects=True, vmem_limit_bytes=60 * 1024 * 1024
        ),
    )(activations, w, ow)


def solution(mesh):
    return jax.shard_map(
        shards,
        mesh=mesh,
        in_specs=(P(None, "row", "col"), P(None, None, "row", "col"), P("row", "col", None)),
        out_specs=P(None, "col", "row"),
        check_vma=False,
    )
```

time: 446 us -> 106 us (0.24)
  waiting for transfers between devices: 358 us -> 0 us
  Pallas kernels: 0 us -> 104 us
  matrix products: 25.9 us -> 0 us
  starting transfers between devices: 25.6 us -> 0 us
  between operations: 13.2 us -> 0.01 us
  blocking collectives: 9.27 us -> 0 us
  other arithmetic: 5.3 us -> 0 us
  local copies, waits for them, and re-layouts: 6.59 us -> 1.64 us
    all_gather x2 -> x0, waiting for transfers between devices: 280 us -> none  [the longest x1 149 us: shards(): lax.all_gather(normed, 'row', axis=1, tiled=True)]
    pallas_call x0 -> x1, Pallas kernels: none -> 104 us  [shards(): pl.pallas_call(kernel, out_shape=jax.ShapeDtypeStruct((NX, 64, NOUT), F32...]
    all_to_all x2 -> x0, waiting for transfers between devices: 35.1 us -> none  [the longest x1 22.2 us: shards(): lax.all_to_all(keyvals, 'row', split_axis=0, concat_axis=2, tiled=True)]
    dot_general x5 -> x0, matrix products: 25.9 us -> none  [the longest x1 11.9 us: shards(): jnp.einsum('kqd,knd->kqn', shard_rows, tables, precision=highest)]
    all_to_all x2 -> x0, starting transfers between devices: 25.2 us -> none  [the longest x1 18.7 us: shards(): lax.all_to_all(queries, 'row', split_axis=0, concat_axis=2, tiled=True)]
    unnamed x5 -> x0, waiting for transfers between devices: 21.7 us -> none
    reduce_scatter x1 -> x0, waiting for transfers between devices: 21 us -> none  [shards(): lax.psum_scatter(partial_value, 'col', scatter_dimension=3, tiled=True)]
    psum x1 -> x0, blocking collectives: 9.27 us -> none  [shards(): lax.psum((jnp.sum(activations, -1, keepdims=True), jnp.sum(activations *...]
  transfers between devices with their start and end apart: 6 -> 0, of which waited for: 6 -> 0; matrix products, arithmetic and copies ran while one was open for 1% -> 0% of each run, Pallas kernels for 0% -> 0%
where the time goes in v4:
time: 106 us
  Pallas kernels  104 us (98%)
  local copies, waits for them, and re-layouts  1.64 us (2%)
    pallas_call x1, Pallas kernels, shards(): pl.pallas_call(kernel, out_shape=jax.ShapeDtypeStruct((NX, 64, NOUT), F32...  104 us

profile of v4, /device:TPU:1, one launch (start us, length us, event | category | flops | bytes accessed | tf_op | source)
XLA Modules:
  0.0 105.5 jit_solution(1740266647056241223)
XLA Ops:
  0.0 103.9 %shard_map.37 = f32[4,64,48]{2,1,0:T(8,128)} custom-call(f32[4,2,1536]{2,1,0:T(2,128)} %act.1, f32[1152,128]{1,0:T(8,128)} %bitcast.2, f32[384,128]{1,0:T(8,128)} %bitcast.3), custom_call_target="tpu_custom_call" | custom-call | tf_op jit(solution)/shard_map/pallas_call | solution.py:661
  103.9 1.6 %copy.4 = f32[4,64,48]{1,2,0:T(8,128)} copy(f32[4,64,48]{2,1,0:T(8,128)} %shard_map.37) | data formatting | bytes 98304 | tf_op jit(solution)/shard_map/pallas_call | solution.py:661

commit v5 on v4

--- a/solution.py
+++ b/solution.py
@@ -16,12 +16,13 @@
 TILES = 48
 KT = TILES // NX
 R = 2 * TILES
-R1, R2 = 64, 32
+R1, R2 = 72, 24
 STRAIGHT = 7
-STREAMS = 4
+STREAMS = 2
+PER = STREAMS // 2
 HEADS = 32
 NZZ = 8
-A1 = 80
+A1 = 104
 FEAT = 96
 NOUT = 48
 
@@ -44,7 +45,6 @@
     me = y * NZ + z
     near, far = c == 1, c == 0
     even, odd = z % 2 == 0, z % 2 == 1
-    zz0 = z // 2
 
     def dev(yy, zz, cc, xx):
         return ((yy * NZ + zz) * 2 + cc, xx)
@@ -137,14 +137,22 @@
 
         lax.fori_loop(0, KT, body, 0)
 
+    def ysplit(q, n):
+        share = (n // 2 + 7) // 8 * 8
+        return pl.ds(share, n - share) if q else pl.ds(0, share)
+
     def core(piece, sem, sent):
-        remote(piece, piece, sent, sem, dev(y, z, 0, x))
+        remote(piece, piece, sent, sem, to_far)
+
+    def place(d, s):
+        return (NZ - s) % NZ if d else s
 
     def back(d, s):
         return wrap(z - s, NZ) if d == 0 else wrap(z + s, NZ)
 
-    def onward(d, k):
-        return dev(y, wrap(z + k, NZ) if d == 0 else wrap(z - k, NZ), 1, x)
+    toward = [dev(y, wrap(z + 1, NZ), 1, x), dev(y, wrap(z - 1, NZ), 1, x)]
+    to_yp, to_ym, to_yo = [dev(yy, z, 1, x) for yy in (yp, ym, yo)]
+    to_far = dev(y, z, 0, x)
 
     ONES = pl.ds(0, R1)
     TWOS = pl.ds(R1, R2)
@@ -156,34 +164,32 @@
         return pl.ds(first + share, n - share) if d else pl.ds(first, share)
 
     def z1piece(u, d, s, t):
-        n = R1 // 2
-        return g.at[back(d, s - t), y, u // 2, cutting(d, s, u % 2 * n, n)]
+        n = R1 // PER
+        return g.at[place(d, s - t), y, u // PER, cutting(d, s, u % PER * n, n)]
 
     def z2piece(u, d, s, t):
-        return g.at[back(d, s - t), pl.ds(u % 2 * 2, 2), u // 2, cutting(d, s, R1, R2)]
+        return g.at[place(d, s - t), pl.ds(u % PER * (NY // PER), NY // PER), u // PER, cutting(d, s, R1, R2)]
 
     def z1(u, d, s):
-        piece = z1piece(u, d, s, 1)
-        remote(piece, piece, z1_s, r1.at[u, d, s - 1], onward(d, 1))
+        remote(z1piece(u, d, s, 1), z1piece(u, d, s, 0), z1_s, r1.at[u, d, s - 1], toward[d])
 
     def z2(u, d, s):
-        piece = z2piece(u, d, s, 1)
-        remote(piece, piece, z2_s, r2.at[u, d, s - 1], onward(d, 1))
+        remote(z2piece(u, d, s, 1), z2piece(u, d, s, 0), z2_s, r2.at[u, d, s - 1], toward[d])
 
     def y1(slot, straight):
         piece = g.at[slot, y, :, ONES]
-        remote(piece, piece, y_s, ry.at[0, slot], dev(yp, z, 1, x))
-        remote(piece, piece, y_s, ry.at[1, slot], dev(ym, z, 1, x))
+        remote(piece, piece, y_s, ry.at[0, slot], to_yp)
+        remote(piece, piece, y_s, ry.at[1, slot], to_ym)
         if straight:
-            remote(piece, piece, y_s, rh.at[0, slot], dev(yo, z, 1, x))
+            remote(piece, piece, y_s, rh.at[0, slot], to_yo)
         core(piece, rc.at[slot], c_s)
 
     def y1pass(slot, straight):
-        for q, origin, target in ((0, ym, yp), (1, yp, ym)):
+        for q, origin, target in ((0, ym, to_yp), (1, yp, to_ym)):
             wait(g.at[slot, origin, :, ONES], ry.at[q, slot])
             if not straight:
-                piece = g.at[slot, origin, :, pl.ds(q * (R1 // 2), R1 // 2)]
-                remote(piece, piece, h_s, rh.at[q, slot], dev(target, z, 1, x))
+                piece = g.at[slot, origin, :, ysplit(q, R1)]
+                remote(piece, piece, h_s, rh.at[q, slot], target)
         core(g.at[slot, ym, :, ONES], rc.at[slot], c_s)
         core(g.at[slot, yp, :, ONES], rc.at[slot], c_s)
 
@@ -192,13 +198,11 @@
             wait(g.at[slot, yo, :, ONES], rh.at[0, slot])
         else:
             for q in range(2):
-                wait(g.at[slot, yo, :, pl.ds(q * (R1 // 2), R1 // 2)], rh.at[q, slot])
+                wait(g.at[slot, yo, :, ysplit(q, R1)], rh.at[q, slot])
         core(g.at[slot, yo, :, ONES], rc.at[slot], c_s)
 
     def spots(s):
-        if s in (0, NZ // 2):
-            return [(back(0, s), s >= STRAIGHT)]
-        return [(back(d, s), s >= STRAIGHT) for d in range(2)]
+        return [(p, s >= STRAIGHT) for p in sorted({place(d, s) for d in range(2)})]
 
     @pl.when(near)
     def _():
@@ -217,20 +221,20 @@
             normed = (data - center) * scale
             for t in range(TILES):
                 v = normed[t // KT, :, t % KT * LANE : (t % KT + 1) * LANE]
-                g[z, y, cls, pl.ds(2 * t, 2), :] = v
-            for u in (2 * cls, 2 * cls + 1):
+                g[0, y, cls, pl.ds(2 * t, 2), :] = v
+            for u in range(PER * cls, PER * cls + PER):
                 for d in range(2):
                     z1(u, d, 1)
-        own2 = g.at[z, y, :, TWOS]
-        for k, target in enumerate((yp, ym, yo)):
-            remote(own2, own2, p_s, rp.at[k], dev(target, z, 1, x))
-        y1(z, False)
+        own2 = g.at[0, y, :, TWOS]
+        for k, target in enumerate((to_yp, to_ym, to_yo)):
+            remote(own2, own2, p_s, rp.at[k], target)
+        y1(0, False)
         for k, origin in enumerate((ym, yp, yo)):
-            wait(g.at[z, origin, :, TWOS], rp.at[k])
+            wait(g.at[0, origin, :, TWOS], rp.at[k])
         for u in range(STREAMS):
             for d in range(2):
                 z2(u, d, 1)
-        core(g.at[z, :, :, TWOS], rc.at[z], c2_s)
+        core(g.at[0, :, :, TWOS], rc.at[0], c2_s)
         last = NZ // 2
         for s in range(1, last + 4):
             if s <= last:
@@ -290,13 +294,14 @@
 
         def arrive(k, carry):
             away = (k + 1) // 2
-            slot = wrap(z + away - 2 * away * (k % 2), NZ)
-            wait(g.at[slot], rc.at[slot])
+            lies = away + (NZ - 2 * away) * (k % 2)
+            slot = wrap(z - away + 2 * away * (k % 2), NZ)
+            wait(g.at[lies], rc.at[lies])
             rows = pl.ds(pl.multiple_of(slot * 16, 16), 16)
             low = pl.ds(pl.multiple_of(2 * LANE + slot * 16, 16), 16)
             for t in range(TILES):
                 v = jnp.concatenate(
-                    [flat_g[pl.ds(slot * (NY * NC * R) + 2 * t + b, NY * NC, stride=R), :] for b in range(2)], 0
+                    [flat_g[pl.ds(lies * (NY * NC * R) + 2 * t + b, NY * NC, stride=R), :] for b in range(2)], 0
                 )
                 hi, lo = split(v)
                 lanes = pl.ds(t % KT * LANE, LANE)
@@ -329,8 +334,11 @@
                     ]
 
         def post(k, carry):
-            h = (k + me // 2) % HEADS
-            there = h // NZZ * NZ + h % NZZ * 2
+            j = k // NY
+            zz = (z // 2 + 4 + (j + 1) // 2 * (1 - 2 * (j % 2))) % NZZ
+            yy = (y + 2 + k) % NY
+            h = yy * NZZ + zz
+            there = yy * NZ + zz * 2
             rows = pl.ds(pl.multiple_of(h * 8, 8), 8)
             dst = rcv.at[pl.ds(pl.multiple_of(me * 8, 8), 8)]
             remote(msg.at[1, rows], dst, a2a_s, a2a_r, (there * 2 + 1, x))
@@ -402,44 +410,42 @@
             for k in range(2)
         )
         for d2 in range(2):
-            att[zz0, y, c, pl.ds(d2, 64, stride=2), :] = o[d2 * 64 : d2 * 64 + 64]
-
-    def slot_of(d, s):
-        return back(d, s) // 2
+            att[0, y, c, pl.ds(d2, 64, stride=2), :] = o[d2 * 64 : d2 * 64 + 64]
+
+    def lies(d, s):
+        return place(d, s) // 2
 
     def b1piece(u, d, s, t):
-        n = A1 // 2
-        return att.at[slot_of(d, s - t), y, u // 2, cutting(d, s, u % 2 * n, n)]
+        n = A1 // PER
+        return att.at[lies(d, s - t), y, u // PER, cutting(d, s, u % PER * n, n)]
 
     def b2piece(u, d, s, t):
-        return att.at[slot_of(d, s - t), pl.ds(u % 2 * 2, 2), u // 2, cutting(d, s, A1, LANE - A1)]
+        return att.at[lies(d, s - t), pl.ds(u % PER * (NY // PER), NY // PER), u // PER, cutting(d, s, A1, LANE - A1)]
 
     def b1(u, d, s):
-        piece = b1piece(u, d, s, 1)
-        remote(piece, piece, z1_s, r1.at[u, d, s - 1], onward(d, 1))
+        remote(b1piece(u, d, s, 1), b1piece(u, d, s, 0), z1_s, r1.at[u, d, s - 1], toward[d])
 
     def b2(u, d, s):
-        piece = b2piece(u, d, s, 1)
-        remote(piece, piece, z2_s, r2.at[u, d, s - 1], onward(d, 1))
+        remote(b2piece(u, d, s, 1), b2piece(u, d, s, 0), z2_s, r2.at[u, d, s - 1], toward[d])
 
     FIRST = pl.ds(0, A1)
     SECOND = pl.ds(A1, LANE - A1)
 
     def v1(slot, straight, own=False):
         piece = att.at[slot, y, :, FIRST]
-        remote(piece, piece, y_s, ry.at[0, slot], dev(yp, z, 1, x))
-        remote(piece, piece, y_s, ry.at[1, slot], dev(ym, z, 1, x))
+        remote(piece, piece, y_s, ry.at[0, slot], to_yp)
+        remote(piece, piece, y_s, ry.at[1, slot], to_ym)
         if straight:
-            remote(piece, piece, y_s, rh.at[0, slot], dev(yo, z, 1, x))
+            remote(piece, piece, y_s, rh.at[0, slot], to_yo)
         if not own:
             core(piece, rc.at[slot], c_s)
 
     def v1pass(slot, straight):
-        for q, origin, target in ((0, ym, yp), (1, yp, ym)):
+        for q, origin, target in ((0, ym, to_yp), (1, yp, to_ym)):
             wait(att.at[slot, origin, :, FIRST], ry.at[q, slot])
             if not straight:
-                piece = att.at[slot, origin, :, pl.ds(q * (A1 // 2), A1 // 2)]
-                remote(piece, piece, h_s, rh.at[q, slot], dev(target, z, 1, x))
+                piece = att.at[slot, origin, :, ysplit(q, A1)]
+                remote(piece, piece, h_s, rh.at[q, slot], target)
         core(att.at[slot, ym, :, FIRST], rc.at[slot], c_s)
         core(att.at[slot, yp, :, FIRST], rc.at[slot], c_s)
 
@@ -448,13 +454,11 @@
             wait(att.at[slot, yo, :, FIRST], rh.at[0, slot])
         else:
             for q in range(2):
-                wait(att.at[slot, yo, :, pl.ds(q * (A1 // 2), A1 // 2)], rh.at[q, slot])
+                wait(att.at[slot, yo, :, ysplit(q, A1)], rh.at[q, slot])
         core(att.at[slot, yo, :, FIRST], rc.at[slot], c_s)
 
     def places(s):
-        if s in (0, NZ // 2):
-            return [(slot_of(0, s), s >= STRAIGHT)]
-        return [(slot_of(d, s), s >= STRAIGHT) for d in range(2)]
+        return [(p, s >= STRAIGHT) for p in sorted({lies(d, s) for d in range(2)})]
 
     ACROSS = pl.ds(0, 2 * NOUT)
 
@@ -462,8 +466,8 @@
     def _():
         acc[ACROSS] = jnp.zeros((2 * NOUT, 4 * LANE), F32)
 
-    def finish(slot):
-        halves = [split(att[slot, :, cls].reshape(NY * LANE, LANE)) for cls in range(2)]
+    def finish(p, slot):
+        halves = [split(att[p, :, cls].reshape(NY * LANE, LANE)) for cls in range(2)]
         hi = jnp.concatenate([h for h, _ in halves], 1)
         lo = jnp.concatenate([l for _, l in halves], 1)
         acc[ACROSS] += jnp.dot(
@@ -500,22 +504,22 @@
 
     @pl.when(near & even)
     def _():
-        core(att.at[zz0, y, 1], rc.at[zz0], c_s)
-        wait(att.at[zz0, y, 0], b_r)
+        core(att.at[0, y, 1], rc.at[0], c_s)
+        wait(att.at[0, y, 0], b_r)
         for u in range(STREAMS):
             for d in range(2):
                 b1(u, d, 1)
-        own = att.at[zz0, y, :, SECOND]
-        for k, target in enumerate((yp, ym, yo)):
-            remote(own, own, p_s, rp.at[k], dev(target, z, 1, x))
-        v1(zz0, False, True)
+        own = att.at[0, y, :, SECOND]
+        for k, target in enumerate((to_yp, to_ym, to_yo)):
+            remote(own, own, p_s, rp.at[k], target)
+        v1(0, False, True)
         for k, origin in enumerate((ym, yp, yo)):
-            wait(att.at[zz0, origin, :, SECOND], rp.at[k])
+            wait(att.at[0, origin, :, SECOND], rp.at[k])
         for u in range(STREAMS):
             for d in range(2):
                 b2(u, d, 1)
         for origin in (ym, yp, yo):
-            core(att.at[zz0, origin, :, SECOND], rc.at[zz0], c_s)
+            core(att.at[0, origin, :, SECOND], rc.at[0], c_s)
         round_of(2, places(0), [])
         round_of(4, places(2), places(0))
         round_of(6, places(4), places(2))
@@ -530,26 +534,27 @@
         round_of(7, places(5), places(3))
         last_of(places(7), places(5) + places(7))
 
-    def from_near(slot):
-        wait(att.at[slot], rc.at[slot])
-        finish(slot)
+    def from_near(s):
+        for d in range(1 if s in (0, NZ // 2) else 2):
+            p = lies(d, s)
+            if s:
+                wait(att.at[p], rc.at[p])
+            else:
+                drain(rc.at[p], (2 * NY - 1) * LANE)
+            finish(p, back(d, s) // 2)
 
     @pl.when(far & even)
     def _():
-        own = att.at[zz0, y, 0]
+        own = att.at[0, y, 0]
         remote(own, own, b_s, b_r, dev(y, z, 1, x))
-        drain(rc.at[zz0], (2 * NY - 1) * LANE)
-        finish(zz0)
-        for s in (2, 4, 6, 8):
-            for slot, _ in places(s):
-                from_near(slot)
+        for s in (0, 2, 4, 6, 8):
+            from_near(s)
         wait(own, b_s)
 
     @pl.when(far & odd)
     def _():
         for s in (1, 3, 5, 7):
-            for slot, _ in places(s):
-                from_near(slot)
+            from_near(s)
 
     @pl.when(far)
     def _():
@@ -618,8 +623,7 @@
 
     @pl.when(near & odd)
     def _():
-        up, down = 24, 16
-        drain(z1_s, NC * (2 * 3 * A1 + 2 * up + 2 * down))
+        drain(z1_s, NC * 7 * A1)
         drain(z2_s, NC * 7 * NY * (LANE - A1))
         drain(y_s, (NZZ * 2 + 2) * 2 * A1)
         drain(h_s, (NZZ - 2) * 2 * A1)

time: 106 us -> 104 us (0.981)
  Pallas kernels: 104 us -> 102 us
    pallas_call x1, Pallas kernels: 104 us -> 102 us  [shards(): pl.pallas_call(kernel, out_shape=jax.ShapeDtypeStruct((NX, 64, NOUT), F32...]
where the time goes in v5:
time: 104 us
  Pallas kernels  102 us (98%)
  local copies, waits for them, and re-layouts  1.64 us (2%)
    pallas_call x1, Pallas kernels, shards(): pl.pallas_call(kernel, out_shape=jax.ShapeDtypeStruct((NX, 64, NOUT), F32...  102 us

profile of v5, /device:TPU:1, one launch (start us, length us, event | category | flops | bytes accessed | tf_op | source)
XLA Modules:
  0.0 104.0 jit_solution(2927073626771452829)
XLA Ops:
  0.0 102.4 %shard_map.37 = f32[4,64,48]{2,1,0:T(8,128)} custom-call(f32[4,2,1536]{2,1,0:T(2,128)} %act.1, f32[1152,128]{1,0:T(8,128)} %bitcast.2, f32[384,128]{1,0:T(8,128)} %bitcast.3), custom_call_target="tpu_custom_call" | custom-call | tf_op jit(solution)/shard_map/pallas_call | solution.py:665
  102.4 1.6 %copy.4 = f32[4,64,48]{1,2,0:T(8,128)} copy(f32[4,64,48]{2,1,0:T(8,128)} %shard_map.37) | data formatting | bytes 98304 | tf_op jit(solution)/shard_map/pallas_call | solution.py:665

commit v6 on v5

--- a/solution.py
+++ b/solution.py
@@ -236,7 +236,7 @@
                 z2(u, d, 1)
         core(g.at[0, :, :, TWOS], rc.at[0], c2_s)
         last = NZ // 2
-        for s in range(1, last + 4):
+        for s in range(1, last + 3):
             if s <= last:
                 for u in range(STREAMS):
                     for d in range(2):
@@ -254,11 +254,11 @@
                             z2(u, d, t + 1)
                 for slot, _ in spots(t):
                     core(g.at[slot, :, :, TWOS], rc.at[slot], c2_s)
+            if 0 <= s - 1 <= last:
+                for spot in spots(s - 1):
+                    y1pass(*spot)
             if 0 <= s - 2 <= last:
                 for spot in spots(s - 2):
-                    y1pass(*spot)
-            if 0 <= s - 3 <= last:
-                for spot in spots(s - 3):
                     y1last(*spot)
 
     @pl.when(far)

time: 104 us -> 102 us (0.981)
  Pallas kernels: 102 us -> 100 us
    pallas_call x1, Pallas kernels: 102 us -> 100 us  [shards(): pl.pallas_call(kernel, out_shape=jax.ShapeDtypeStruct((NX, 64, NOUT), F32...]
where the time goes in v6:
time: 102 us
  Pallas kernels  100 us (98%)
  local copies, waits for them, and re-layouts  1.64 us (2%)
    pallas_call x1, Pallas kernels, shards(): pl.pallas_call(kernel, out_shape=jax.ShapeDtypeStruct((NX, 64, NOUT), F32...  100 us

profile of v6, /device:TPU:1, one launch (start us, length us, event | category | flops | bytes accessed | tf_op | source)
XLA Modules:
  0.0 102.0 jit_solution(14198037475263912135)
XLA Ops:
  0.0 100.3 %shard_map.37 = f32[4,64,48]{2,1,0:T(8,128)} custom-call(f32[4,2,1536]{2,1,0:T(2,128)} %act.1, f32[1152,128]{1,0:T(8,128)} %bitcast.2, f32[384,128]{1,0:T(8,128)} %bitcast.3), custom_call_target="tpu_custom_call" | custom-call | tf_op jit(solution)/shard_map/pallas_call | solution.py:665
  100.4 1.6 %copy.4 = f32[4,64,48]{1,2,0:T(8,128)} copy(f32[4,64,48]{2,1,0:T(8,128)} %shard_map.37) | data formatting | bytes 98304 | tf_op jit(solution)/shard_map/pallas_call | solution.py:665

commit v7 on v6

--- a/solution.py
+++ b/solution.py
@@ -20,6 +20,7 @@
 STRAIGHT = 7
 STREAMS = 2
 PER = STREAMS // 2
+EARLY = 9
 HEADS = 32
 NZZ = 8
 A1 = 104
@@ -284,12 +285,6 @@
         gather_send(ow, ob, 0, OH, o_s, o_r)
         wait(ob.at[1, x], on_r)
         gather_send(ob.at[1, x], ob, 1, OH, o_s, o_r)
-        for d2 in range(2):
-            for q in range(2):
-                gather_last(wb, d2, WH, q, wf_r)
-                wconv(d2, xo, q)
-        own.wait()
-
         flat_g = g.reshape(NZ * NY * NC * R, LANE)
 
         def arrive(k, carry):
@@ -309,7 +304,18 @@
                 ghl[t // KT, low, lanes] = lo
             return carry
 
-        lax.fori_loop(0, NZ, arrive, 0)
+        lax.fori_loop(0, EARLY, arrive, 0)
+        for d2 in range(2):
+            for q in range(2):
+                gather_last(wb, d2, WH, q, wf_r)
+                wconv(d2, xo, q)
+        own.wait()
+
+        lax.fori_loop(EARLY, NZ, arrive, 0)
+        for p in range(2):
+            for d2 in range(2):
+                gather_pass(ob, d2, OH, 0, p, o_s, o_r, of_r)
+                gather_pass(ob, d2, OH, 1, 1 - p, o_s, o_r, of_r)
 
         acc[...] = jnp.zeros_like(acc)
         turned = (((1,), (1,)), ((), ()))
@@ -355,10 +361,6 @@
 
         lax.fori_loop(0, HEADS, post, 0)
 
-        for p in range(2):
-            for d2 in range(2):
-                gather_pass(ob, d2, OH, 0, p, o_s, o_r, of_r)
-                gather_pass(ob, d2, OH, 1, 1 - p, o_s, o_r, of_r)
         for d2 in range(2):
             for q in range(2):
                 gather_last(ob, d2, OH, q, of_r)

time: 102 us -> 102 us (level)
  no operation moved by 1% of the time
where the time goes in v7:
time: 102 us
  Pallas kernels  100 us (98%)
  local copies, waits for them, and re-layouts  1.64 us (2%)
    pallas_call x1, Pallas kernels, shards(): pl.pallas_call(kernel, out_shape=jax.ShapeDtypeStruct((NX, 64, NOUT), F32...  100 us

profile of v7, /device:TPU:1, one launch (start us, length us, event | category | flops | bytes accessed | tf_op | source)
XLA Modules:
  0.0 102.1 jit_solution(520259183908158544)
XLA Ops:
  0.0 100.4 %shard_map.37 = f32[4,64,48]{2,1,0:T(8,128)} custom-call(f32[4,2,1536]{2,1,0:T(2,128)} %act.1, f32[1152,128]{1,0:T(8,128)} %bitcast.2, f32[384,128]{1,0:T(8,128)} %bitcast.3), custom_call_target="tpu_custom_call" | custom-call | tf_op jit(solution)/shard_map/pallas_call | solution.py:667
  100.4 1.6 %copy.4 = f32[4,64,48]{1,2,0:T(8,128)} copy(f32[4,64,48]{2,1,0:T(8,128)} %shard_map.37) | data formatting | bytes 98304 | tf_op jit(solution)/shard_map/pallas_call | solution.py:667
